TPU v7x, 32 devices: a whole 2x2x4 slice. The times are simulated.
32 devices in a mesh: row: 8 (over y, x, core), col: 4 (over z).
Axes of the slice: x: 2, y: 2, z: 4, core: 2. Of those that a mesh axis runs over, the one named last changes fastest.
Arguments:
- inputs: bfloat16 [256, 12288], P('col', 'row'), may hold values from -6 to 6
- w_up: bfloat16 [12288, 24576], P('row', 'col'), may hold values from -0.0546875 to 0.0546875
- w_down: bfloat16 [24576, 12288], P('col', 'row'), may hold values from -0.0390625 to 0.0390625
- mask_up: int32 [96, 192], P('row', 'col'), may hold values from 0 to 1, as said below
- mask_down: int32 [192, 96], P('col', 'row'), may hold values from 0 to 1, as said below
- cotangent: bfloat16 [256, 12288], P('col', 'row'), may hold values from -1.5 to 1.5
Outputs:
- outputs: bfloat16 [256, 12288], P('col', 'row')
- grad_inputs: bfloat16 [256, 12288], P('col', 'row')
- grad_up: bfloat16 [12288, 24576], P('row', 'col')
- grad_down: bfloat16 [24576, 12288], P('col', 'row')
Inputs may be any that keep to these rules, and one draw needn't show every extreme that they name: `mask_up`: each entry is 0 or 1; the chance of a 1 is the same along a row of tiles and differs from row to row, between 0.2 and 0.8. `mask_down`: each entry is 0 or 1; the chance of a 1 is the same along a row of tiles and differs from row to row, between 0.2 and 0.8.
All inputs are finite; a program needn't handle non-finite values.
Results may differ from a plain program's by a relative error of at most 0.029.
Values may be sent and summed in bfloat16 or wider, within the bound.
No kernel may reach another device: no remote copies, remote signals or barrier semaphores. Data moves between devices by JAX's collectives and lax.ppermute only.
A program may use at most 256 MiB of HBM per device.

v0:
```python
import functools

import jax
import jax.numpy as jnp
from jax import lax
from jax.experimental import pallas as pl
from jax.experimental.pallas import tpu as pltpu
from jax.sharding import PartitionSpec as P

TILE = 128
VMEM_LIMIT = 11 << 20
PIECE = 256
F32 = jnp.float32
BF16 = jnp.bfloat16


def smooth_gate(value):
    return jax.nn.gelu(value, approximate=True)


def contract(left, right, left_dim, right_dim):
    return lax.dot_general(
        left, right, (((left_dim,), (right_dim,)), ((), ())), preferred_element_type=F32
    )


def apply_mask(weight, mask):
    rows, cols = mask.shape
    tile = weight.shape[0] // rows
    shaped = weight.reshape(rows, tile, cols, tile)
    keep = mask[:, None, :, None].astype(weight.dtype)
    return (shaped * keep).reshape(weight.shape)


def activate(hidden, grad_act):
    act = smooth_gate(hidden).astype(BF16)
    _, pull = jax.vjp(smooth_gate, hidden)
    grad_hidden = pull(grad_act)[0].astype(BF16)
    return (act, grad_hidden)


def per_device_plain(inputs, w_up, w_down, mask_up, mask_down, cotangent):
    up_kept = apply_mask(w_up, mask_up)
    down_kept = apply_mask(w_down, mask_down)
    inputs_all, cot_all = (
        lax.all_gather(inputs, "col", axis=0, tiled=True),
        lax.all_gather(cotangent, "col", axis=0, tiled=True),
    )
    up_part = jnp.dot(inputs_all, up_kept, preferred_element_type=F32)
    back_part = contract(cot_all, down_kept, 1, 1)
    hidden, grad_act = (
        lax.psum_scatter(
            part.astype(BF16), "row", scatter_dimension=0, tiled=True
        ).astype(F32)
        for part in (up_part, back_part)
    )
    act, grad_hidden = activate(hidden, grad_act)
    act_all, grad_all = (
        lax.all_gather(act, "row", axis=0, tiled=True),
        lax.all_gather(grad_hidden, "row", axis=0, tiled=True),
    )
    out_part = jnp.dot(act_all, down_kept, preferred_element_type=F32)
    input_part = contract(grad_all, up_kept, 1, 1)
    outputs, grad_inputs = (
        lax.psum_scatter(
            part.astype(BF16), "col", scatter_dimension=0, tiled=True
        ).astype(F32)
        for part in (out_part, input_part)
    )
    grad_down = apply_mask(contract(act_all, cot_all, 0, 0).astype(BF16), mask_down)
    grad_up = apply_mask(contract(inputs_all, grad_all, 0, 0).astype(BF16), mask_up)
    return (outputs.astype(BF16), grad_inputs.astype(BF16), grad_up, grad_down)


CORE, X, Y = 1, 2, 4


def first_of(row):
    return X if row % 2 == 0 else Y


AT_SENT, AT_HELD, AT_NEAR, AT_FAR = 0, 4, 8, 12
AT_NEAR_CORE, AT_FAR_CORE = 10, 14


def share_table(row):
    first = jnp.where(row % 2 == 0, X, Y)
    second = (X | Y) - first
    other = row ^ CORE
    sent = [other ^ first ^ second, other ^ second, other ^ first, other]
    held = [row ^ first ^ second, row ^ first, row ^ second, row]
    near = [row, row ^ first, other, other ^ second]
    far = [row ^ second, row ^ second ^ first, other ^ first, other ^ first ^ second]
    return jnp.stack(sent + held + near + far)


def cost(flops, moved):
    return pl.CostEstimate(flops=int(flops) // 1000, bytes_accessed=int(moved) // 1000, transcendentals=0)


def params():
    return pltpu.CompilerParams(
        dimension_semantics=("arbitrary",), vmem_limit_bytes=VMEM_LIMIT
    )


def whole(array):
    return pl.BlockSpec(array.shape, lambda i, t: (0,) * len(array.shape))


def resident():
    return pl.BlockSpec(memory_space=pltpu.VMEM)


def in_vmem(array):
    return pltpu.with_memory_space_constraint(array, pltpu.VMEM)


def flat(parts):
    return [array for part in parts for array in part]


def parts_of(refs, parts):
    refs = iter(refs)
    return [functools.reduce(jnp.add, [next(refs)[...] for _ in part]) for part in parts]


def stack(dst, values):
    row = 0
    for value in values:
        dst[row : row + value.shape[0], :] = value
        row += value.shape[0]


def small(body, outs, *given):
    specs = tuple(resident() for _ in outs)
    return pl.pallas_call(
        body,
        out_shape=tuple(pltpu.VMEM(shape, dtype) for shape, dtype in outs),
        in_specs=[resident()] * len(given),
        out_specs=specs,
        compiler_params=pltpu.CompilerParams(vmem_limit_bytes=VMEM_LIMIT),
    )(*[in_vmem(array) for array in given])


def add_cores(held, got):
    _, tokens, share = held.shape

    def body(held_ref, got_ref, pair, rest):
        for k in range(4):
            total = held_ref[k].astype(F32) + got_ref[k].astype(F32)
            if k < 2:
                pair[k] = total.astype(BF16)
            else:
                rest[k - 2] = total

    shape = (2, tokens, share)
    return small(body, [(shape, BF16), (shape, F32)], held, got)


def add_first(rest, near):
    _, tokens, share = rest.shape

    def body(rest_ref, near_ref, passed, own):
        passed[...] = (rest_ref[0] + near_ref[0].astype(F32)).astype(BF16)
        own[...] = rest_ref[1] + near_ref[1].astype(F32)

    return small(body, [((tokens, share), BF16), ((tokens, share), F32)], rest, near)


def activated(own, last):
    def body(own_ref, last_ref, hidden, act):
        value = own_ref[...] + last_ref[...].astype(F32)
        hidden[...] = value
        act[...] = smooth_gate(value).astype(BF16)

    return small(body, [(own.shape, F32), (own.shape, BF16)], own, last)


def pulled(hidden, own, last):
    def body(hidden_ref, own_ref, last_ref, grad):
        _, pull = jax.vjp(smooth_gate, hidden_ref[...])
        grad[...] = pull(own_ref[...] + last_ref[...].astype(F32))[0].astype(BF16)

    return small(body, [(own.shape, BF16)], hidden, own, last)[0]


def paired(left, right):
    def body(left_ref, right_ref, pair):
        pair[0] = left_ref[...]
        pair[1] = right_ref[...]

    return small(body, [((2,) + left.shape, BF16)], left, right)[0]


def added(terms):
    def body(*refs):
        *given, out = refs
        out[...] = functools.reduce(jnp.add, [ref[...].astype(F32) for ref in given]).astype(BF16)

    return pl.pallas_call(
        body,
        out_shape=jax.ShapeDtypeStruct(terms[0].shape, BF16),
        compiler_params=pltpu.CompilerParams(vmem_limit_bytes=VMEM_LIMIT),
    )(*terms)


def kept_pieces(weight, keep, shares, by_rows, pieces):
    rows, columns = weight.shape
    share = (rows if by_rows else columns) // shares
    block = (share, PIECE) if by_rows else (PIECE, share)

    def body(weight_ref, keep_ref, *refs):
        *outs, sems = refs

        def copies(n):
            start = pl.multiple_of(n * share, TILE)
            for h, lo in enumerate(pieces):
                if by_rows:
                    source = weight_ref.at[pl.ds(start, share), pl.ds(lo, PIECE)]
                else:
                    source = weight_ref.at[pl.ds(lo, PIECE), pl.ds(start, share)]
                yield pltpu.make_async_copy(source, outs[h].at[n], sems.at[n, h])

        for n in range(shares):
            for copy in copies(n):
                copy.start()

        @pl.loop(0, shares)
        def _(n):
            for copy in copies(n):
                copy.wait()
            for lo, out in zip(pieces, outs):
                for k in range(0, block[0], TILE):
                    strip = slice(k, k + TILE)
                    if by_rows:
                        kept = keep_ref[n, k // TILE : k // TILE + 1, lo : lo + PIECE]
                    else:
                        tile = (lo + k) // TILE
                        kept = keep_ref[n, tile : tile + 1, :]
                    out[n, strip, :] = out[n, strip, :] * kept

    return pl.pallas_call(
        body,
        out_shape=(pltpu.VMEM((shares,) + block, BF16),) * len(pieces),
        in_specs=[pl.BlockSpec(memory_space=pltpu.HBM), resident()],
        out_specs=(resident(),) * len(pieces),
        scratch_shapes=[pltpu.SemaphoreType.DMA((shares, len(pieces)))],
        compiler_params=pltpu.CompilerParams(vmem_limit_bytes=VMEM_LIMIT),
        cost_estimate=cost(rows * columns, 4 * rows * columns),
    )(pltpu.with_memory_space_constraint(weight, pltpu.HBM), keep)


def share_block(kept_refs, share, by_rows):
    return jnp.concatenate([ref[share] for ref in kept_refs], axis=1 if by_rows else 0)


def project(table, ats, parts, kept, by_rows):
    tokens = sum(part[0].shape[0] for part in parts)
    wide = parts[0][0].shape[1]
    share = kept[0].shape[1 if by_rows else 2]
    count = len(flat(parts))

    def body(table_ref, *refs):
        part_refs, refs = refs[:count], refs[count:]
        kept_refs, (*outs, held) = refs[: len(kept)], refs[len(kept) :]
        i = pl.program_id(0)

        @pl.when(i == 0)
        def _():
            stack(held, parts_of(part_refs, parts))

        right = share_block(kept_refs, table_ref[ats[0] + i], by_rows)
        result = contract(held[...], right, 1, 1 if by_rows else 0).astype(BF16)
        for n, out in enumerate(outs):

            @pl.when(i // 4 == n)
            def _(out=out):
                out[...] = result

    def place(n):
        return lambda i, t: (jnp.clip(i - 4 * n, 0, 3), 0, 0)

    call = pl.pallas_call(
        body,
        out_shape=(jax.ShapeDtypeStruct((4, tokens, share), BF16),) * len(ats),
        grid_spec=pltpu.PrefetchScalarGridSpec(
            num_scalar_prefetch=1,
            grid=(4 * len(ats),),
            in_specs=[whole(array) for array in flat(parts)] + [resident()] * len(kept),
            out_specs=tuple(
                pl.BlockSpec((None, tokens, share), place(n)) for n in range(len(ats))
            ),
            scratch_shapes=[pltpu.VMEM((tokens, wide), BF16)],
        ),
        compiler_params=params(),
        cost_estimate=cost(
            8 * tokens * wide * share * len(ats),
            2 * (4 * len(ats) * share * (wide + tokens) + tokens * wide),
        ),
    )
    return call(table, *flat(parts), *map(in_vmem, kept))


def fetch(i, pairs, refs, held, sems):
    copies = [
        pltpu.make_async_copy(ref, held.at[pl.ds(2 * n, 2)], sems.at[n])
        for n, ref in enumerate(refs)
    ]

    @pl.when(i == 0)
    def _():
        for copy in copies:
            copy.start()

    for n, copy in enumerate(copies):

        @pl.when(i == 2 * n)
        def _(copy=copy):
            copy.wait()


def gathered(table, at, pairs, kept, by_rows, base=None, blocks=0):
    _, tokens, share = pairs[0].shape
    steps = 2 * len(pairs)
    wide = len(kept) * PIECE
    total_shape = (tokens, wide)
    given = [] if base is None else [base]

    def body(table_ref, *refs):
        pair_refs, refs = refs[: len(pairs)], refs[len(pairs) :]
        kept_refs, refs = refs[: len(kept)], refs[len(kept) :]
        base_refs, refs = refs[: len(given)], refs[len(given) :]
        if blocks:
            *outs, total, held, sems = refs
        else:
            total, held, sems = refs
        i = pl.program_id(0)
        fetch(i, pairs, pair_refs, held, sems)

        @pl.when(i == 0)
        def _():
            total[...] = base_refs[0][...] if given else jnp.zeros(total_shape, F32)

        right = share_block(kept_refs, table_ref[at + i], by_rows)
        total[...] += contract(held[i], right, 1, 0 if by_rows else 1)

        if blocks:

            @pl.when(i == steps - 1)
            def _():
                rows = tokens // blocks
                for k, out in enumerate(outs):
                    out[...] = total[k * rows : (k + 1) * rows, :].astype(BF16)

    scratch = [
        pltpu.VMEM((steps, tokens, share), BF16),
        pltpu.SemaphoreType.DMA((len(pairs),)),
    ]
    if blocks:
        out_shape = (jax.ShapeDtypeStruct((tokens // blocks, wide), BF16),) * blocks
        out_specs = (whole(out_shape[0]),) * blocks
        scratch.insert(0, pltpu.VMEM(total_shape, F32))
    else:
        out_shape = jax.ShapeDtypeStruct(total_shape, F32)
        out_specs = whole(out_shape)
    call = pl.pallas_call(
        body,
        out_shape=out_shape,
        grid_spec=pltpu.PrefetchScalarGridSpec(
            num_scalar_prefetch=1,
            grid=(steps,),
            in_specs=[pl.BlockSpec(memory_space=pl.ANY)] * len(pairs)
            + [resident()] * len(kept)
            + [whole(array) for array in given],
            out_specs=out_specs,
            scratch_shapes=scratch,
        ),
        compiler_params=params(),
        cost_estimate=cost(
            2 * tokens * share * wide * steps,
            2 * share * (wide + tokens) * steps + 4 * tokens * wide,
        ),
    )
    return call(table, *pairs, *map(in_vmem, kept), *given)


def weight_gradient(table, at, pairs, parts, keep, shape, by_rows, into=None):
    tokens = sum(part[0].shape[0] for part in parts)
    share = pairs[0].shape[2]
    wide = parts[0][0].shape[1]
    count = len(flat(parts))
    steps = 2 * len(pairs)
    block = (share, wide) if by_rows else (wide, share)
    given = [] if into is None else [into]

    def body(table_ref, *refs):
        pair_refs, refs = refs[: len(pairs)], refs[len(pairs) :]
        part_refs, refs = refs[:count], refs[count:]
        keep_ref, *_, out, made, held, other, sems, out_sems = refs
        i = pl.program_id(0)
        slot = i % 2

        def copy(step):
            start = pl.multiple_of(table_ref[at + step] * share, TILE)
            if by_rows:
                target = out.at[pl.ds(start, share)]
            else:
                target = out.at[:, pl.ds(start, share)]
            return pltpu.make_async_copy(made.at[step % 2], target, out_sems.at[step % 2])

        @pl.when(i == 0)
        def _():
            values = parts_of(part_refs, parts)
            if by_rows:
                stack(other, values)
            else:
                other[...] = jnp.concatenate(values).T

        fetch(i, pairs, pair_refs, held, sems)

        @pl.when(i >= 2)
        def _():
            copy(i - 2).wait()

        left = held[i].T if by_rows else other
        right = other[...] if by_rows else held[i]
        span = 2 * TILE
        for lo in range(0, block[0], span):
            term = contract(left[lo : lo + span, :], right, 1, 0)
            for k in range(0, span, TILE):
                tile = (lo + k) // TILE
                made[slot, lo + k : lo + k + TILE, :] = (
                    term[k : k + TILE].astype(BF16) * keep_ref[tile : tile + 1, :]
                )
        copy(i).start()

        @pl.when(i == steps - 1)
        def _():
            copy(i - 1).wait()
            copy(i).wait()

    call = pl.pallas_call(
        body,
        out_shape=jax.ShapeDtypeStruct(shape, BF16),
        grid_spec=pltpu.PrefetchScalarGridSpec(
            num_scalar_prefetch=1,
            grid=(steps,),
            in_specs=[pl.BlockSpec(memory_space=pl.ANY)] * len(pairs)
            + [whole(array) for array in flat(parts)]
            + [pl.BlockSpec((None,) + keep.shape[1:], lambda i, t: (t[at + i], 0, 0))]
            + [pl.BlockSpec(memory_space=pl.ANY)] * len(given),
            out_specs=pl.BlockSpec(memory_space=pl.ANY),
            scratch_shapes=[
                pltpu.VMEM((2,) + block, BF16),
                pltpu.VMEM((steps, tokens, share), BF16),
                pltpu.VMEM((tokens, wide) if by_rows else (wide, tokens), BF16),
                pltpu.SemaphoreType.DMA((len(pairs),)),
                pltpu.SemaphoreType.DMA((2,)),
            ],
        ),
        input_output_aliases={2 + len(pairs) + count: 0} if given else {},
        compiler_params=params(),
        cost_estimate=cost(
            2 * tokens * share * wide * steps, 2 * share * (wide + tokens) * steps
        ),
    )
    return call(table, *pairs, *flat(parts), keep, *given)


def per_device_tuned(n_row, n_col, inputs, w_up, w_down, mask_up, mask_down, cotangent):
    share = w_up.shape[1] // n_row
    table = share_table(lax.axis_index("row"))
    keep_up = jnp.repeat(mask_up.astype(BF16), TILE, axis=1)
    keep_up = keep_up.reshape(-1, n_row, share).transpose(1, 0, 2)
    keep_down = jnp.repeat(mask_down.astype(BF16), TILE, axis=1)
    keep_down = keep_down.reshape(n_row, share // TILE, -1)

    def between_cores(value):
        return lax.ppermute(value, "row", [(i, i ^ CORE) for i in range(n_row)])

    def along_first(value):
        return lax.ppermute(value, "row", [(i, i ^ first_of(i)) for i in range(n_row)])

    def along_second(value):
        second = [(X | Y) - first_of(i) for i in range(n_row)]
        return lax.ppermute(value, "row", [(i, i ^ second[i]) for i in range(n_row)])

    def along_col(value, shift):
        return lax.ppermute(value, "col", [(i, (i + shift) % n_col) for i in range(n_col)])

    def toward(value, step, froms):
        return lax.ppermute(value, "col", [(i, i + step) for i in froms])

    def relayed(lower, upper):
        return toward(upper, -1, (1, 2)), toward(lower, 1, (1, 2))

    def after(value, *done):
        return lax.optimization_barrier((value, *done))[0]

    def together(*values):
        return lax.optimization_barrier(values)

    def col_sum(blocks):
        return [blocks[0]] + [along_col(blocks[k], -k) for k in range(1, n_col)]

    features = range(0, w_up.shape[0], PIECE)
    keep_up, keep_down, table = together(keep_up, keep_down, table)
    shifts = [along_col(inputs, k) for k in range(1, n_col)]
    up = kept_pieces(w_up, keep_up, n_row, False, features)
    down = kept_pieces(w_down, after(keep_down, up[0]), n_row, True, features)
    shifts, up, down = together(shifts, up, down)
    inputs_all = [(inputs,)] + [(shift,) for shift in shifts]

    cot = after(cotangent, *shifts)
    lower, upper = along_col(cot, 1), along_col(cot, -1)
    up_sent, up_held = project(
        after(table, down[0]), (AT_SENT, AT_HELD), inputs_all, up, False
    )
    lower, upper, up_sent, up_held = together(lower, upper, up_sent, up_held)
    far = relayed(lower, upper)
    pair, rest = add_cores(up_held, between_cores(up_sent))

    near = along_first(pair)
    near, far_lower, far_upper = together(near, *far)
    cot_all = [(cotangent,), (lower,), (far_lower, far_upper), (upper,)]
    passed, own = add_first(rest, near)
    last = along_second(passed)
    back_sent, back_held = project(
        after(table, passed), (AT_SENT, AT_HELD), cot_all, down, True
    )
    last, back_sent, back_held = together(last, back_sent, back_held)
    hidden, act = activated(own, last)

    act_first = along_first(act)
    back_pair, rest = add_cores(after(back_held, act), between_cores(back_sent))
    near = along_first(back_pair)
    act_near = paired(act, after(act_first, back_pair))
    act_far = along_second(act_near)
    act_core = between_cores(act_near)

    def grad_down_of(start, at, pairs, into=None):
        return weight_gradient(
            after(table, start), at, pairs, cot_all, keep_down, w_down.shape, True, into
        )

    grad_down = grad_down_of(act_near, AT_NEAR, [act_near])
    near, grad_down = together(near, grad_down)
    passed, own = add_first(rest, near)
    last = along_second(passed)
    act_core = after(act_core, passed)
    out_total = gathered(table, AT_NEAR, [act_near, act_core], down, True)
    grad_down = grad_down_of(out_total, AT_NEAR_CORE, [act_core], grad_down)
    last, out_total, grad_down = together(last, out_total, grad_down)
    act_far = after(act_far, out_total)
    act_far_core = between_cores(act_far)
    grad = pulled(hidden, own, last)

    grad_first = along_first(grad)
    out_blocks = gathered(
        after(table, grad), AT_FAR, [act_far, act_far_core], down, True, out_total, n_col
    )
    grad_first, *out_blocks = together(grad_first, *out_blocks)
    out_terms = col_sum(out_blocks)
    grad_near = paired(grad, grad_first)
    grad_far = along_second(grad_near)
    grad_core = between_cores(grad_near)
    in_total = gathered(table, AT_NEAR, [grad_near, grad_core], up, False)
    grad_far, in_total, out_terms[1], out_terms[3] = together(
        grad_far, in_total, out_terms[1], out_terms[3]
    )
    grad_far_core = between_cores(grad_far)
    in_total = gathered(table, AT_FAR, [grad_far], up, False, in_total)
    in_blocks = gathered(table, AT_FAR_CORE, [grad_far_core], up, False, in_total, n_col)

    in_terms = col_sum(in_blocks)
    grad_down = grad_down_of(in_blocks[0], AT_FAR, [act_far, act_far_core], grad_down)
    grad_up = weight_gradient(
        after(table, grad_down),
        AT_NEAR,
        [grad_near, grad_core, grad_far, grad_far_core],
        inputs_all,
        keep_up,
        w_up.shape,
        False,
    )
    out_terms[1:] = together(*out_terms[1:], grad_up)[:-1]
    outputs = added(out_terms)
    grad_inputs = added(in_terms)
    return (outputs, grad_inputs, grad_up, grad_down)


def solution(mesh):
    in_specs = (
        P("col", "row"),
        P("row", "col"),
        P("col", "row"),
        P("row", "col"),
        P("col", "row"),
        P("col", "row"),
    )
    out_specs = (P("col", "row"), P("col", "row"), P("row", "col"), P("col", "row"))
    n_row, n_col = mesh.shape["row"], mesh.shape["col"]

    def per_device(inputs, w_up, w_down, mask_up, mask_down, cotangent):
        fits = n_row == 8 and n_col == 4 and mask_up.shape[1] % n_row == 0 and w_up.shape[0] % PIECE == 0
        plan = functools.partial(per_device_tuned, n_row, n_col) if fits else per_device_plain
        return plan(inputs, w_up, w_down, mask_up, mask_down, cotangent)

    return jax.shard_map(
        per_device, mesh=mesh, in_specs=in_specs, out_specs=out_specs, check_vma=False
    )
```

profile of v0, /device:TPU:0, one launch (start us, length us, event | category | flops | bytes accessed | tf_op | source)
XLA Modules:
  0.0 143.8 jit_solution(7178860884453741199)
XLA Ops:
  0.6 5.1 %collective-permute-start.2 = (bf16[64,1536]{1,0:T(8,128)(2,1)}, bf16[64,1536]{1,0:T(8,128)(2,1)S(1)}, u32[]{:S(2)}, u32[]{:S(2)}) collective-permute-start(bf16[64,1536]{1,0:T(8,128)(2,1)} %refs_4_.1), channel_id=1, source_target_pairs={{0,3},{1,0},{2,1},{3,2},{4,7},{5,4},{6,5},{7,6},{8,11},{9,8},{10,9... | collective-permute-start | bytes 589832 | tf_op jit(solution)/shard_map/ppermute | solution.py:490
  9.1 7.0 %shard_map.93 = (bf16[8,256,768]{2,1,0:T(8,128)(2,1)S(1)}, bf16[8,256,768]{2,1,0:T(8,128)(2,1)S(1)}, bf16[8,256,768]{2,1,0:T(8,128)(2,1)S(1)}, bf16[8,256,768]{2...) custom-call(bf16[1536,6144]{1,0:T(8,128)(2,1)} %weight_ref.2, ...), custom_call_target="tpu_custom_call" | custom-call | flops 9437 | bytes 37748 | tf_op jit(solution)/shard_map/pallas_call | solution.py:243
  16.1 7.3 %shard_map.94 = (bf16[8,768,256]{2,1,0:T(8,128)(2,1)S(1)}, bf16[8,768,256]{2,1,0:T(8,128)(2,1)S(1)}, bf16[8,768,256]{2,1,0:T(8,128)(2,1)S(1)}, bf16[8,768,256]{2...) custom-call(bf16[6144,1536]{1,0:T(8,128)(2,1)} %weight_ref.3, ...), custom_call_target="tpu_custom_call" | custom-call | flops 9437 | bytes 37748 | tf_op jit(solution)/shard_map/pallas_call | solution.py:243
  23.4 2.9 %collective-permute-start.4 = (bf16[64,1536]{1,0:T(8,128)(2,1)S(1)}, bf16[64,1536]{1,0:T(8,128)(2,1)S(1)}, u32[]{:S(2)}, u32[]{:S(2)}) collective-permute-start(bf16[64,1536]{1,0:T(8,128)(2,1)S(1)} %copy-done), channel_id=1, source_target_pairs={{0,3},{1,0},{2,1},{3,2},{4,7},{5,4},{6,5},{7,6},{8,11},{9,8},{10,9... | collective-permute-start | bytes 589832 | tf_op jit(solution)/shard_map/ppermute | solution.py:490
  26.3 7.2 %shard_map.95 = (bf16[4,256,768]{2,1,0:T(8,128)(2,1)S(1)}, bf16[4,256,768]{2,1,0:T(8,128)(2,1)S(1)}) custom-call(s32[16]{0:T(128)S(1)} %stack.46.table_ref, bf16[64,1536]{1,0:T(8,128)(2,1)S(1)} %copy-done.1, bf16[64,1536]{1,0:T(8,128)(2,1)S(1)} %collective-permute-done.refs_1_.refs_5_, bf16[64,1536]{1,0:T(8,128)(2,1)S(1)} %collective-permute-done.1.refs_2_.refs_6_, ...), custom_call_target="tpu_custom_call" | custom-call | flops 4831838 | bytes 22806 | tf_op jit(solution)/shard_map/pallas_call | solution.py:302
  35.3 3.4 %collective-permute-done.5.got_ref = bf16[4,256,768]{2,1,0:T(8,128)(2,1)S(1)} collective-permute-done((bf16[4,256,768]{2,1,0:T(8,128)(2,1)S(1)}, bf16[4,256,768]{2,1,0:T(8,128)(2,1)S(1)}, u32[]{:S(2)}, u32[]{:S(2)}) %collective-permute-start.5) | collective-permute-done | bytes 1572896 | tf_op jit(solution)/shard_map/ppermute | solution.py:480
  42.5 6.6 %collective-permute-done.7.refs_2_.refs_3_.refs_4_ = bf16[64,1536]{1,0:T(8,128)(2,1)S(1)} collective-permute-done((bf16[64,1536]{1,0:T(8,128)(2,1)S(1)}, bf16[64,1536]{1,0:T(8,128)(2,1)S(1)}, u32[]{:S(2)}, u32[]{:S(2)}) %collective-permute-start.7) | collective-permute-done | bytes 196640 | tf_op jit(solution)/shard_map/ppermute | solution.py:493
  49.1 1.9 %collective-permute-done.6.near_ref = bf16[2,256,768]{2,1,0:T(8,128)(2,1)S(1)} collective-permute-done((bf16[2,256,768]{2,1,0:T(8,128)(2,1)S(1)}, bf16[2,256,768]{2,1,0:T(8,128)(2,1)S(1)}, u32[]{:S(2)}, u32[]{:S(2)}) %collective-permute-start.6) | collective-permute-done | bytes 786464 | tf_op jit(solution)/shard_map/ppermute | solution.py:483
  52.8 7.5 %shard_map.98 = (bf16[4,256,768]{2,1,0:T(8,128)(2,1)S(1)}, bf16[4,256,768]{2,1,0:T(8,128)(2,1)S(1)}) custom-call(s32[16]{0:T(128)S(1)} %stack.46.table_ref, bf16[64,1536]{1,0:T(8,128)(2,1)S(1)} %copy-done, bf16[64,1536]{1,0:T(8,128)(2,1)S(1)} %collective-permute-done.3.refs_1_.refs_2_.refs_3_, ...), custom_call_target="tpu_custom_call" | custom-call | flops 4831838 | bytes 22806 | tf_op jit(solution)/shard_map/pallas_call | solution.py:302
  65.6 2.9 %collective-permute-done.12.right_ref = bf16[256,768]{1,0:T(8,128)(2,1)S(1)} collective-permute-done((bf16[256,768]{1,0:T(8,128)(2,1)S(1)}, bf16[256,768]{1,0:T(8,128)(2,1)S(1)}, u32[]{:S(2)}, u32[]{:S(2)}) %collective-permute-start.12) | collective-permute-done | bytes 393248 | tf_op jit(solution)/shard_map/ppermute | solution.py:483
  69.2 3.7 %shard_map.102.refs_7_ = bf16[6144,1536]{1,0:T(8,128)(2,1)} custom-call(s32[16]{0:T(128)S(1)} %stack.46.table_ref, bf16[2,256,768]{2,1,0:T(8,128)(2,1)S(1)} %shard_map.101.refs_0_, bf16[64,1536]{1,0:T(8,128)(2,1)S(1)} %copy-done, bf16[64,1536]{1,0:T(8,128)(2,1)S(1)} %collective-permute-done.3.refs_1_.refs_2_.refs_3_, ...), custom_call_target="tpu_custom_call" | custom-call | flops 1207959 | bytes 5505 | tf_op jit(solution)/shard_map/pallas_call | solution.py:468
  73.0 9.1 %collective-permute-done.11.near_ref = bf16[2,256,768]{2,1,0:T(8,128)(2,1)S(1)} collective-permute-done((bf16[2,256,768]{2,1,0:T(8,128)(2,1)S(1)}, bf16[2,256,768]{2,1,0:T(8,128)(2,1)S(1)}, u32[]{:S(2)}, u32[]{:S(2)}) %collective-permute-start.11) | collective-permute-done | bytes 786464 | tf_op jit(solution)/shard_map/ppermute | solution.py:483
  82.8 4.0 %shard_map.104.refs_8_ = f32[256,1536]{1,0:T(8,128)S(1)} custom-call(s32[16]{0:T(128)S(1)} %stack.46.table_ref, bf16[2,256,768]{2,1,0:T(8,128)(2,1)S(1)} %shard_map.101.refs_0_, bf16[2,256,768]{2,1,0:T(8,128)(2,1)S(1)} %collective-permute-done.14.refs_1_.refs_0_, bf16[8,768,256]{2,1,0:T(8,128)(2,1)S(1)} %get-tuple-element.116.refs_5_.refs_2_, ...), custom_call_target="tpu_custom_call" | custom-call | flops 2415919 | bytes 12582 | tf_op jit(solution)/shard_map/pallas_call | solution.py:385
  86.8 3.7 %shard_map.105.refs_8_ = bf16[6144,1536]{1,0:T(8,128)(2,1)} custom-call(s32[16]{0:T(128)S(1)} %stack.46.table_ref, bf16[2,256,768]{2,1,0:T(8,128)(2,1)S(1)} %collective-permute-done.14.refs_1_.refs_0_, bf16[64,1536]{1,0:T(8,128)(2,1)S(1)} %copy-done, ...), custom_call_target="tpu_custom_call", output_to_operand_aliasing={{}: (8, {})} | custom-call | flops 1207959 | bytes 5505 | tf_op jit(solution)/shard_map/pallas_call | solution.py:468
  92.9 4.1 %shard_map.107 = (bf16[64,1536]{1,0:T(8,128)(2,1)S(1)}, bf16[64,1536]{1,0:T(8,128)(2,1)S(1)}, bf16[64,1536]{1,0:T(8,128)(2,1)S(1)}, bf16[64,1536]{1,0:T(8,128)(2,1)S(1)}) custom-call(s32[16]{0:T(128)S(1)} %stack.46.table_ref, bf16[2,256,768]{2,1,0:T(8,128)(2,1)S(1)} %collective-permute-done.16.refs_0_, ...), custom_call_target="tpu_custom_call" | custom-call | flops 2415919 | bytes 12582 | tf_op jit(solution)/shard_map/pallas_call | solution.py:385
  96.9 2.1 %collective-permute-done.15.right_ref = bf16[256,768]{1,0:T(8,128)(2,1)S(1)} collective-permute-done((bf16[256,768]{1,0:T(8,128)(2,1)S(1)}, bf16[256,768]{1,0:T(8,128)(2,1)S(1)}, u32[]{:S(2)}, u32[]{:S(2)}) %collective-permute-start.15) | collective-permute-done | bytes 393248 | tf_op jit(solution)/shard_map/ppermute | solution.py:483
  100.8 2.2 %collective-permute-start.20 = (bf16[64,1536]{1,0:T(8,128)(2,1)S(1)}, bf16[64,1536]{1,0:T(8,128)(2,1)S(1)}, u32[]{:S(2)}, u32[]{:S(2)}) collective-permute-start(bf16[64,1536]{1,0:T(8,128)(2,1)S(1)} %get-tuple-element.171), channel_id=1, source_target_pairs={{0,3},{1,0},{2,1},{3,2},{4,7},{5,4},{6,5},{7,6},{8,11},{9,8},{10,9... | collective-permute-start | bytes 589832 | tf_op jit(solution)/shard_map/ppermute | solution.py:490
  103.0 4.2 %shard_map.109.refs_7_ = f32[256,1536]{1,0:T(8,128)S(1)} custom-call(s32[16]{0:T(128)S(1)} %stack.46.table_ref, bf16[2,256,768]{2,1,0:T(8,128)(2,1)S(1)} %shard_map.108.refs_0_, bf16[2,256,768]{2,1,0:T(8,128)(2,1)S(1)} %collective-permute-done.19.refs_1_, bf16[8,256,768]{2,1,0:T(8,128)(2,1)S(1)} %get-tuple-element.118.refs_4_.refs_2_.refs_1_, ...), custom_call_target="tpu_custom_call" | custom-call | flops 2415919 | bytes 12582 | tf_op jit(solution)/shard_map/pallas_call | solution.py:385
  108.3 5.6 %collective-permute-done.21.refs_3_ = bf16[64,1536]{1,0:T(8,128)(2,1)S(1)} collective-permute-done((bf16[64,1536]{1,0:T(8,128)(2,1)S(1)}, bf16[64,1536]{1,0:T(8,128)(2,1)S(1)}, u32[]{:S(2)}, u32[]{:S(2)}) %collective-permute-start.21) | collective-permute-done | bytes 196640 | tf_op jit(solution)/shard_map/ppermute | solution.py:490
  114.5 2.4 %shard_map.110.refs_7_ = f32[256,1536]{1,0:T(8,128)S(1)} custom-call(s32[16]{0:T(128)S(1)} %stack.46.table_ref, bf16[2,256,768]{2,1,0:T(8,128)(2,1)S(1)} %collective-permute-done.18.refs_0_.refs_2_, bf16[8,256,768]{2,1,0:T(8,128)(2,1)S(1)} %get-tuple-element.118.refs_4_.refs_2_.refs_1_, bf16[8,256,768]{2,1,0:T(8,128)(2,1)S(1)} %get-tuple-element.119.refs_5_.refs_3_.refs_2_, ...), custom_call_target="tpu_custom_call" | custom-call | flops 1207959 | bytes 7077 | tf_op jit(solution)/shard_map/pallas_call | solution.py:385
  116.9 2.5 %shard_map.111 = (bf16[64,1536]{1,0:T(8,128)(2,1)S(1)}, bf16[64,1536]{1,0:T(8,128)(2,1)S(1)}, bf16[64,1536]{1,0:T(8,128)(2,1)S(1)}, bf16[64,1536]{1,0:T(8,128)(2,1)S(1)}) custom-call(s32[16]{0:T(128)S(1)} %stack.46.table_ref, bf16[2,256,768]{2,1,0:T(8,128)(2,1)S(1)} %collective-permute-done.23.refs_0_.refs_3_, ...), custom_call_target="tpu_custom_call" | custom-call | flops 1207959 | bytes 7077 | tf_op jit(solution)/shard_map/pallas_call | solution.py:385
  119.4 2.2 %collective-permute-start.24 = (bf16[64,1536]{1,0:T(8,128)(2,1)S(1)}, bf16[64,1536]{1,0:T(8,128)(2,1)S(1)}, u32[]{:S(2)}, u32[]{:S(2)}) collective-permute-start(bf16[64,1536]{1,0:T(8,128)(2,1)S(1)} %get-tuple-element.185), channel_id=1, source_target_pairs={{0,3},{1,0},{2,1},{3,2},{4,7},{5,4},{6,5},{7,6},{8,11},{9,8},{10,9... | collective-permute-start | bytes 589832 | tf_op jit(solution)/shard_map/ppermute | solution.py:490
  123.8 6.0 %shard_map.112 = bf16[6144,1536]{1,0:T(8,128)(2,1)} custom-call(s32[16]{0:T(128)S(1)} %stack.46.table_ref, bf16[2,256,768]{2,1,0:T(8,128)(2,1)S(1)} %collective-permute-done.16.refs_0_, bf16[2,256,768]{2,1,0:T(8,128)(2,1)S(1)} %collective-permute-done.17.refs_1_, bf16[64,1536]{1,0:T(8,128)(2,1)S(1)} %copy-done, ...), custom_call_target="tpu_custom_call", output_to_operand_aliasing={{}: (9, {})} | custom-call | flops 2415919 | bytes 11010 | tf_op jit(solution)/shard_map/pallas_call | solution.py:468
  129.9 10.7 %shard_map.113 = bf16[1536,6144]{1,0:T(8,128)(2,1)} custom-call(s32[16]{0:T(128)S(1)} %stack.46.table_ref, bf16[2,256,768]{2,1,0:T(8,128)(2,1)S(1)} %shard_map.108.refs_0_, bf16[2,256,768]{2,1,0:T(8,128)(2,1)S(1)} %collective-permute-done.19.refs_1_, bf16[2,256,768]{2,1,0:T(8,128)(2,1)S(1)} %collective-permute-done.18.refs_0_.refs_2_, ...), custom_call_target="tpu_custom_call" | custom-call | flops 4831838 | bytes 22020 | tf_op jit(solution)/shard_map/pallas_call | solution.py:468
  (66 shorter events, 28.6 us)
Async XLA Ops:
  0.6 22.8 %collective-permute-start.2 = (bf16[64,1536]{1,0:T(8,128)(2,1)}, bf16[64,1536]{1,0:T(8,128)(2,1)S(1)}, u32[]{:S(2)}, u32[]{:S(2)}) collective-permute-start(bf16[64,1536]{1,0:T(8,128)(2,1)} %refs_4_.1), channel_id=1, source_target_pairs={{0,3},{1,0},{2,1},{3,2},{4,7},{5,4},{6,5},{7,6},{8,11},{9,8},{10,9... | collective-permute-start | bytes 589832 | tf_op jit(solution)/shard_map/ppermute | solution.py:490
  5.7 17.7 %collective-permute-start.1 = (bf16[64,1536]{1,0:T(8,128)(2,1)}, bf16[64,1536]{1,0:T(8,128)(2,1)S(1)}, u32[]{:S(2)}, u32[]{:S(2)}) collective-permute-start(bf16[64,1536]{1,0:T(8,128)(2,1)} %refs_4_.1), channel_id=1, source_target_pairs={{0,2},{1,3},{2,0},{3,1},{4,6},{5,7},{6,4},{7,5},{8,10},{9,11},{10,... | collective-permute-start | bytes 589832 | tf_op jit(solution)/shard_map/ppermute | solution.py:490
  5.7 17.7 %collective-permute-start = (bf16[64,1536]{1,0:T(8,128)(2,1)}, bf16[64,1536]{1,0:T(8,128)(2,1)S(1)}, u32[]{:S(2)}, u32[]{:S(2)}) collective-permute-start(bf16[64,1536]{1,0:T(8,128)(2,1)} %refs_4_.1), channel_id=1, source_target_pairs={{0,1},{1,2},{2,3},{3,0},{4,5},{5,6},{6,7},{7,4},{8,9},{9,10},{10,1... | collective-permute-start | bytes 589832 | tf_op jit(solution)/shard_map/ppermute | solution.py:490
  23.4 10.1 %collective-permute-start.4 = (bf16[64,1536]{1,0:T(8,128)(2,1)S(1)}, bf16[64,1536]{1,0:T(8,128)(2,1)S(1)}, u32[]{:S(2)}, u32[]{:S(2)}) collective-permute-start(bf16[64,1536]{1,0:T(8,128)(2,1)S(1)} %copy-done), channel_id=1, source_target_pairs={{0,3},{1,0},{2,1},{3,2},{4,7},{5,4},{6,5},{7,6},{8,11},{9,8},{10,9... | collective-permute-start | bytes 589832 | tf_op jit(solution)/shard_map/ppermute | solution.py:490
  26.3 8.9 %collective-permute-start.3 = (bf16[64,1536]{1,0:T(8,128)(2,1)S(1)}, bf16[64,1536]{1,0:T(8,128)(2,1)S(1)}, u32[]{:S(2)}, u32[]{:S(2)}) collective-permute-start(bf16[64,1536]{1,0:T(8,128)(2,1)S(1)} %copy-done), channel_id=1, source_target_pairs={{0,1},{1,2},{2,3},{3,0},{4,5},{5,6},{6,7},{7,4},{8,9},{9,10},{10,1... | collective-permute-start | bytes 589832 | tf_op jit(solution)/shard_map/ppermute | solution.py:490
  39.0 12.1 %collective-permute-start.6 = (bf16[2,256,768]{2,1,0:T(8,128)(2,1)S(1)}, bf16[2,256,768]{2,1,0:T(8,128)(2,1)S(1)}, u32[]{:S(2)}, u32[]{:S(2)}) collective-permute-start(bf16[2,256,768]{2,1,0:T(8,128)(2,1)S(1)} %get-tuple-element.129), channel_id=1, source_target_pairs={{0,8},{4,20},{8,0},{12,28},{16,24},{20,4},{24,16},{28,12},{1,9},{5... | collective-permute-start | bytes 2359304 | tf_op jit(solution)/shard_map/ppermute | solution.py:483
  40.6 8.6 %collective-permute-start.7 = (bf16[64,1536]{1,0:T(8,128)(2,1)S(1)}, bf16[64,1536]{1,0:T(8,128)(2,1)S(1)}, u32[]{:S(2)}, u32[]{:S(2)}) collective-permute-start(bf16[64,1536]{1,0:T(8,128)(2,1)S(1)} %collective-permute-done.4.refs_4_.refs_5_.refs_6_), channel_id=1, source_target_pairs={{1,0},{2,1},{5,4},{6,5},{9,8},{10,9},{13,12},{14,13},{17,16},{18,1... | collective-permute-start | bytes 589832 | tf_op jit(solution)/shard_map/ppermute | solution.py:493
  41.8 7.3 %collective-permute-start.8 = (bf16[64,1536]{1,0:T(8,128)(2,1)S(1)}, bf16[64,1536]{1,0:T(8,128)(2,1)S(1)}, u32[]{:S(2)}, u32[]{:S(2)}) collective-permute-start(bf16[64,1536]{1,0:T(8,128)(2,1)S(1)} %collective-permute-done.3.refs_1_.refs_2_.refs_3_), channel_id=1, source_target_pairs={{1,2},{2,3},{5,6},{6,7},{9,10},{10,11},{13,14},{14,15},{17,18},{18... | collective-permute-start | bytes 589832 | tf_op jit(solution)/shard_map/ppermute | solution.py:493
  51.2 9.1 %collective-permute-start.9 = (bf16[256,768]{1,0:T(8,128)(2,1)S(1)}, bf16[256,768]{1,0:T(8,128)(2,1)S(1)}, u32[]{:S(2)}, u32[]{:S(2)}) collective-permute-start(bf16[256,768]{1,0:T(8,128)(2,1)S(1)} %get-tuple-element.134), channel_id=1, source_target_pairs={{0,16},{4,12},{8,24},{12,4},{16,0},{20,28},{24,8},{28,20},{1,17},{... | collective-permute-start | bytes 1179656 | tf_op jit(solution)/shard_map/ppermute | solution.py:487
  60.3 3.5 %collective-permute-start.10 = (bf16[4,256,768]{2,1,0:T(8,128)(2,1)S(1)}, bf16[4,256,768]{2,1,0:T(8,128)(2,1)S(1)}, u32[]{:S(2)}, u32[]{:S(2)}) collective-permute-start(bf16[4,256,768]{2,1,0:T(8,128)(2,1)S(1)} %get-tuple-element.150), channel_id=1, source_target_pairs={{0,4},{4,0},{8,12},{12,8},{16,20},{20,16},{24,28},{28,24},{1,5},{5... | collective-permute-start | bytes 4718600 | tf_op jit(solution)/shard_map/ppermute | solution.py:480
  60.7 7.8 %collective-permute-start.12 = (bf16[256,768]{1,0:T(8,128)(2,1)S(1)}, bf16[256,768]{1,0:T(8,128)(2,1)S(1)}, u32[]{:S(2)}, u32[]{:S(2)}) collective-permute-start(bf16[256,768]{1,0:T(8,128)(2,1)S(1)} %get-tuple-element.148.left_ref), channel_id=1, source_target_pairs={{0,8},{4,20},{8,0},{12,28},{16,24},{20,4},{24,16},{28,12},{1,9},{5... | collective-permute-start | bytes 1179656 | tf_op jit(solution)/shard_map/ppermute | solution.py:483
  64.1 18.0 %collective-permute-start.11 = (bf16[2,256,768]{2,1,0:T(8,128)(2,1)S(1)}, bf16[2,256,768]{2,1,0:T(8,128)(2,1)S(1)}, u32[]{:S(2)}, u32[]{:S(2)}) collective-permute-start(bf16[2,256,768]{2,1,0:T(8,128)(2,1)S(1)} %get-tuple-element.152), channel_id=1, source_target_pairs={{0,8},{4,20},{8,0},{12,28},{16,24},{20,4},{24,16},{28,12},{1,9},{5... | collective-permute-start | bytes 2359304 | tf_op jit(solution)/shard_map/ppermute | solution.py:483
  68.6 14.2 %collective-permute-start.14 = (bf16[2,256,768]{2,1,0:T(8,128)(2,1)S(1)}, bf16[2,256,768]{2,1,0:T(8,128)(2,1)S(1)}, u32[]{:S(2)}, u32[]{:S(2)}) collective-permute-start(bf16[2,256,768]{2,1,0:T(8,128)(2,1)S(1)} %shard_map.101.refs_0_), channel_id=1, source_target_pairs={{0,4},{4,0},{8,12},{12,8},{16,20},{20,16},{24,28},{28,24},{1,5},{5... | collective-permute-start | bytes 2359304 | tf_op jit(solution)/shard_map/ppermute | solution.py:480
  68.6 21.9 %collective-permute-start.16 = (bf16[2,256,768]{2,1,0:T(8,128)(2,1)S(1)}, bf16[2,256,768]{2,1,0:T(8,128)(2,1)S(1)}, u32[]{:S(2)}, u32[]{:S(2)}) collective-permute-start(bf16[2,256,768]{2,1,0:T(8,128)(2,1)S(1)} %shard_map.101.refs_0_), channel_id=1, source_target_pairs={{0,16},{4,12},{8,24},{12,4},{16,0},{20,28},{24,8},{28,20},{1,17},{... | collective-permute-start | bytes 2359304 | tf_op jit(solution)/shard_map/ppermute | solution.py:487
  82.2 8.3 %collective-permute-start.13 = (bf16[256,768]{1,0:T(8,128)(2,1)S(1)}, bf16[256,768]{1,0:T(8,128)(2,1)S(1)}, u32[]{:S(2)}, u32[]{:S(2)}) collective-permute-start(bf16[256,768]{1,0:T(8,128)(2,1)S(1)} %get-tuple-element.157), channel_id=1, source_target_pairs={{0,16},{4,12},{8,24},{12,4},{16,0},{20,28},{24,8},{28,20},{1,17},{... | collective-permute-start | bytes 1179656 | tf_op jit(solution)/shard_map/ppermute | solution.py:487
  91.2 7.8 %collective-permute-start.15 = (bf16[256,768]{1,0:T(8,128)(2,1)S(1)}, bf16[256,768]{1,0:T(8,128)(2,1)S(1)}, u32[]{:S(2)}, u32[]{:S(2)}) collective-permute-start(bf16[256,768]{1,0:T(8,128)(2,1)S(1)} %shard_map.106.left_ref), channel_id=1, source_target_pairs={{0,8},{4,20},{8,0},{12,28},{16,24},{20,4},{24,16},{28,12},{1,9},{5... | collective-permute-start | bytes 1179656 | tf_op jit(solution)/shard_map/ppermute | solution.py:483
  99.1 3.9 %collective-permute-start.19 = (bf16[2,256,768]{2,1,0:T(8,128)(2,1)S(1)}, bf16[2,256,768]{2,1,0:T(8,128)(2,1)S(1)}, u32[]{:S(2)}, u32[]{:S(2)}) collective-permute-start(bf16[2,256,768]{2,1,0:T(8,128)(2,1)S(1)} %shard_map.108.refs_0_), channel_id=1, source_target_pairs={{0,4},{4,0},{8,12},{12,8},{16,20},{20,16},{24,28},{28,24},{1,5},{5... | collective-permute-start | bytes 2359304 | tf_op jit(solution)/shard_map/ppermute | solution.py:480
  99.2 14.8 %collective-permute-start.18 = (bf16[2,256,768]{2,1,0:T(8,128)(2,1)S(1)}, bf16[2,256,768]{2,1,0:T(8,128)(2,1)S(1)}, u32[]{:S(2)}, u32[]{:S(2)}) collective-permute-start(bf16[2,256,768]{2,1,0:T(8,128)(2,1)S(1)} %shard_map.108.refs_0_), channel_id=1, source_target_pairs={{0,16},{4,12},{8,24},{12,4},{16,0},{20,28},{24,8},{28,20},{1,17},{... | collective-permute-start | bytes 2359304 | tf_op jit(solution)/shard_map/ppermute | solution.py:487
  100.8 7.5 %collective-permute-start.20 = (bf16[64,1536]{1,0:T(8,128)(2,1)S(1)}, bf16[64,1536]{1,0:T(8,128)(2,1)S(1)}, u32[]{:S(2)}, u32[]{:S(2)}) collective-permute-start(bf16[64,1536]{1,0:T(8,128)(2,1)S(1)} %get-tuple-element.171), channel_id=1, source_target_pairs={{0,3},{1,0},{2,1},{3,2},{4,7},{5,4},{6,5},{7,6},{8,11},{9,8},{10,9... | collective-permute-start | bytes 589832 | tf_op jit(solution)/shard_map/ppermute | solution.py:490
  103.0 11.0 %collective-permute-start.21 = (bf16[64,1536]{1,0:T(8,128)(2,1)S(1)}, bf16[64,1536]{1,0:T(8,128)(2,1)S(1)}, u32[]{:S(2)}, u32[]{:S(2)}) collective-permute-start(bf16[64,1536]{1,0:T(8,128)(2,1)S(1)} %get-tuple-element.172), channel_id=1, source_target_pairs={{0,1},{1,2},{2,3},{3,0},{4,5},{5,6},{6,7},{7,4},{8,9},{9,10},{10,1... | collective-permute-start | bytes 589832 | tf_op jit(solution)/shard_map/ppermute | solution.py:490
  113.9 26.6 %collective-permute-start.22 = (bf16[64,1536]{1,0:T(8,128)(2,1)S(1)}, bf16[64,1536]{1,0:T(8,128)(2,1)S(1)}, u32[]{:S(2)}, u32[]{:S(2)}) collective-permute-start(bf16[64,1536]{1,0:T(8,128)(2,1)S(1)} %get-tuple-element.174), channel_id=1, source_target_pairs={{0,2},{1,3},{2,0},{3,1},{4,6},{5,7},{6,4},{7,5},{8,10},{9,11},{10,... | collective-permute-start | bytes 589832 | tf_op jit(solution)/shard_map/ppermute | solution.py:490
  119.4 21.9 %collective-permute-start.24 = (bf16[64,1536]{1,0:T(8,128)(2,1)S(1)}, bf16[64,1536]{1,0:T(8,128)(2,1)S(1)}, u32[]{:S(2)}, u32[]{:S(2)}) collective-permute-start(bf16[64,1536]{1,0:T(8,128)(2,1)S(1)} %get-tuple-element.185), channel_id=1, source_target_pairs={{0,3},{1,0},{2,1},{3,2},{4,7},{5,4},{6,5},{7,6},{8,11},{9,8},{10,9... | collective-permute-start | bytes 589832 | tf_op jit(solution)/shard_map/ppermute | solution.py:490
  121.6 21.4 %collective-permute-start.25 = (bf16[64,1536]{1,0:T(8,128)(2,1)S(1)}, bf16[64,1536]{1,0:T(8,128)(2,1)S(1)}, u32[]{:S(2)}, u32[]{:S(2)}) collective-permute-start(bf16[64,1536]{1,0:T(8,128)(2,1)S(1)} %get-tuple-element.186), channel_id=1, source_target_pairs={{0,2},{1,3},{2,0},{3,1},{4,6},{5,7},{6,4},{7,5},{8,10},{9,11},{10,... | collective-permute-start | bytes 589832 | tf_op jit(solution)/shard_map/ppermute | solution.py:490
  122.7 20.4 %collective-permute-start.26 = (bf16[64,1536]{1,0:T(8,128)(2,1)S(1)}, bf16[64,1536]{1,0:T(8,128)(2,1)S(1)}, u32[]{:S(2)}, u32[]{:S(2)}) collective-permute-start(bf16[64,1536]{1,0:T(8,128)(2,1)S(1)} %get-tuple-element.187), channel_id=1, source_target_pairs={{0,1},{1,2},{2,3},{3,0},{4,5},{5,6},{6,7},{7,4},{8,9},{9,10},{10,1... | collective-permute-start | bytes 589832 | tf_op jit(solution)/shard_map/ppermute | solution.py:490
  (5 other events, 26.3 us)
where the time goes:
time: 144 us
  Pallas kernels  73.7 us (51%)
  waiting for transfers between devices  37.9 us (26%)
  starting transfers between devices  29 us (20%)
    pallas_call x4, Pallas kernels, weight_gradient(): return call(table, *pairs, *flat(parts), keep, *given)  24.1 us
    pallas_call x5, Pallas kernels, gathered(): return call(table, *pairs, *map(in_vmem, kept), *given)  17.1 us
    ppermute x11, starting transfers between devices, along_col(): lax.ppermute(value, 'col', [(i, (i + shift) % n_col) for i in range(n_col)])  16.2 us
    ppermute x4, waiting for transfers between devices, along_first(): lax.ppermute(value, 'row', [(i, i ^ first_of(i)) for i in range(n_row)])  16 us
    pallas_call x2, Pallas kernels, project(): return call(table, *flat(parts), *map(in_vmem, kept))  14.7 us
    pallas_call x2, Pallas kernels, kept_pieces(): pl.pallas_call(body, out_shape=(pltpu.VMEM((shares,) + block, BF16),) * l...  14.3 us
    ppermute x11, waiting for transfers between devices, along_col(): lax.ppermute(value, 'col', [(i, (i + shift) % n_col) for i in range(n_col)])  10.2 us
    ppermute x2, waiting for transfers between devices, toward(): return lax.ppermute(value, 'col', [(i, i + step) for i in froms])  6.61 us
  transfers between devices with their start and end apart: 27, of which 12 were waited for; matrix products, arithmetic and copies ran while one was open for 2% of the time, Pallas kernels for 50%

commit v1 on v0

--- a/solution.py
+++ b/solution.py
@@ -81,6 +81,11 @@
 
 AT_SENT, AT_HELD, AT_NEAR, AT_FAR = 0, 4, 8, 12
 AT_NEAR_CORE, AT_FAR_CORE = 10, 14
+
+
+def spans(length):
+    span = 2 * TILE if length % (2 * TILE) == 0 else TILE
+    return [slice(lo, lo + span) for lo in range(0, length, span)]
 
 
 def share_table(row):
@@ -191,6 +196,16 @@
         pair[1] = right_ref[...]
 
     return small(body, [((2,) + left.shape, BF16)], left, right)[0]
+
+
+def added_pairs(*pairs):
+    def body(*refs):
+        given, outs = refs[: 2 * len(pairs)], refs[2 * len(pairs) :]
+        for n, out in enumerate(outs):
+            left, right = given[2 * n : 2 * n + 2]
+            out[...] = (left[...].astype(F32) + right[...].astype(F32)).astype(BF16)
+
+    return small(body, [(left.shape, BF16) for left, _ in pairs], *flat(pairs))
 
 
 def added(terms):
@@ -424,15 +439,16 @@
             copy(i - 2).wait()
 
         left = held[i].T if by_rows else other
-        right = other[...] if by_rows else held[i]
-        span = 2 * TILE
+        right = other if by_rows else held.at[i]
+        span = share if block[0] % share == 0 else TILE
         for lo in range(0, block[0], span):
-            term = contract(left[lo : lo + span, :], right, 1, 0)
-            for k in range(0, span, TILE):
-                tile = (lo + k) // TILE
-                made[slot, lo + k : lo + k + TILE, :] = (
-                    term[k : k + TILE].astype(BF16) * keep_ref[tile : tile + 1, :]
-                )
+            for columns in spans(block[1]):
+                term = contract(left[lo : lo + span, :], right[:, columns], 1, 0)
+                for k in range(0, span, TILE):
+                    tile = (lo + k) // TILE
+                    made[slot, lo + k : lo + k + TILE, columns] = (
+                        term[k : k + TILE].astype(BF16) * keep_ref[tile : tile + 1, columns]
+                    )
         copy(i).start()
 
         @pl.when(i == steps - 1)
@@ -518,8 +534,9 @@
         after(table, down[0]), (AT_SENT, AT_HELD), inputs_all, up, False
     )
     lower, upper, up_sent, up_held = together(lower, upper, up_sent, up_held)
+    up_got = between_cores(up_sent)
     far = relayed(lower, upper)
-    pair, rest = add_cores(up_held, between_cores(up_sent))
+    pair, rest = add_cores(up_held, up_got)
 
     near = along_first(pair)
     near, far_lower, far_upper = together(near, *far)
@@ -561,14 +578,17 @@
         after(table, grad), AT_FAR, [act_far, act_far_core], down, True, out_total, n_col
     )
     grad_first, *out_blocks = together(grad_first, *out_blocks)
-    out_terms = col_sum(out_blocks)
+    hops = toward(out_blocks[2], 1, (0, 1)), toward(out_blocks[2], -1, (2, 3))
     grad_near = paired(grad, grad_first)
     grad_far = along_second(grad_near)
     grad_core = between_cores(grad_near)
     in_total = gathered(table, AT_NEAR, [grad_near, grad_core], up, False)
-    grad_far, in_total, out_terms[1], out_terms[3] = together(
-        grad_far, in_total, out_terms[1], out_terms[3]
-    )
+    *hops, in_total = together(*hops, in_total)
+    to_upper, to_lower = added_pairs((out_blocks[3], hops[0]), (out_blocks[1], hops[1]))
+    grad_far, in_total, to_upper, to_lower = together(
+        grad_far, in_total, to_upper, to_lower
+    )
+    out_terms = [out_blocks[0], along_col(to_upper, 1), along_col(to_lower, -1)]
     grad_far_core = between_cores(grad_far)
     in_total = gathered(table, AT_FAR, [grad_far], up, False, in_total)
     in_blocks = gathered(table, AT_FAR_CORE, [grad_far_core], up, False, in_total, n_col)

time: 144 us -> 143 us (level)
  waiting for transfers between devices: 37.9 us -> 31.6 us
  starting transfers between devices: 29 us -> 33.5 us
    ppermute x11 -> x10, waiting for transfers between devices: 10.2 us -> 2.34 us  [along_col(): lax.ppermute(value, 'col', [(i, (i + shift) % n_col) for i in range(n_col)])]
    ppermute x2 -> x4, starting transfers between devices: 1.95 us -> 6.55 us  [toward(): return lax.ppermute(value, 'col', [(i, i + step) for i in froms])]
    ppermute x2 -> x4, waiting for transfers between devices: 6.61 us -> 6.84 us  [toward(): return lax.ppermute(value, 'col', [(i, i + step) for i in froms])]
    ppermute x11 -> x10, starting transfers between devices: 16.2 us -> 16.2 us  [along_col(): lax.ppermute(value, 'col', [(i, (i + shift) % n_col) for i in range(n_col)])]
  transfers between devices with their start and end apart: 27 -> 28, of which waited for: 12 -> 12; matrix products, arithmetic and copies ran while one was open for 2% -> 2% of each run, Pallas kernels for 50% -> 51%
where the time goes in v1:
time: 143 us; the launch traced here: 142 us
  Pallas kernels  73.8 us (52%)
  starting transfers between devices  33.5 us (23%)
  waiting for transfers between devices  31.6 us (22%)
    pallas_call x4, Pallas kernels, weight_gradient(): return call(table, *pairs, *flat(parts), keep, *given)  24.1 us
    pallas_call x5, Pallas kernels, gathered(): return call(table, *pairs, *map(in_vmem, kept), *given)  17.1 us
    ppermute x10, starting transfers between devices, along_col(): lax.ppermute(value, 'col', [(i, (i + shift) % n_col) for i in range(n_col)])  16.2 us
    ppermute x4, waiting for transfers between devices, along_first(): lax.ppermute(value, 'row', [(i, i ^ first_of(i)) for i in range(n_row)])  16 us
    pallas_call x2, Pallas kernels, project(): return call(table, *flat(parts), *map(in_vmem, kept))  14.7 us
    pallas_call x2, Pallas kernels, kept_pieces(): pl.pallas_call(body, out_shape=(pltpu.VMEM((shares,) + block, BF16),) * l...  14.3 us
    ppermute x4, waiting for transfers between devices, toward(): return lax.ppermute(value, 'col', [(i, i + step) for i in froms])  6.84 us
    ppermute x4, starting transfers between devices, toward(): return lax.ppermute(value, 'col', [(i, i + step) for i in froms])  6.55 us
  transfers between devices with their start and end apart: 28, of which 12 were waited for; matrix products, arithmetic and copies ran while one was open for 2% of the time, Pallas kernels for 51%

profile of v1, /device:TPU:0, one launch (start us, length us, event | category | flops | bytes accessed | tf_op | source)
XLA Modules:
  0.0 142.2 jit_solution(6441555300019346214)
XLA Ops:
  0.6 5.1 %collective-permute-start.2 = (bf16[64,1536]{1,0:T(8,128)(2,1)}, bf16[64,1536]{1,0:T(8,128)(2,1)S(1)}, u32[]{:S(2)}, u32[]{:S(2)}) collective-permute-start(bf16[64,1536]{1,0:T(8,128)(2,1)} %refs_4_.1), channel_id=1, source_target_pairs={{0,3},{1,0},{2,1},{3,2},{4,7},{5,4},{6,5},{7,6},{8,11},{9,8},{10,9... | collective-permute-start | bytes 589832 | tf_op jit(solution)/shard_map/ppermute | solution.py:506
  9.1 7.0 %shard_map.93 = (bf16[8,256,768]{2,1,0:T(8,128)(2,1)S(1)}, bf16[8,256,768]{2,1,0:T(8,128)(2,1)S(1)}, bf16[8,256,768]{2,1,0:T(8,128)(2,1)S(1)}, bf16[8,256,768]{2...) custom-call(bf16[1536,6144]{1,0:T(8,128)(2,1)} %weight_ref.2, ...), custom_call_target="tpu_custom_call" | custom-call | flops 9437 | bytes 37748 | tf_op jit(solution)/shard_map/pallas_call | solution.py:258
  16.1 7.3 %shard_map.94 = (bf16[8,768,256]{2,1,0:T(8,128)(2,1)S(1)}, bf16[8,768,256]{2,1,0:T(8,128)(2,1)S(1)}, bf16[8,768,256]{2,1,0:T(8,128)(2,1)S(1)}, bf16[8,768,256]{2...) custom-call(bf16[6144,1536]{1,0:T(8,128)(2,1)} %weight_ref.3, ...), custom_call_target="tpu_custom_call" | custom-call | flops 9437 | bytes 37748 | tf_op jit(solution)/shard_map/pallas_call | solution.py:258
  23.5 2.9 %collective-permute-start.4 = (bf16[64,1536]{1,0:T(8,128)(2,1)S(1)}, bf16[64,1536]{1,0:T(8,128)(2,1)S(1)}, u32[]{:S(2)}, u32[]{:S(2)}) collective-permute-start(bf16[64,1536]{1,0:T(8,128)(2,1)S(1)} %copy-done), channel_id=1, source_target_pairs={{0,3},{1,0},{2,1},{3,2},{4,7},{5,4},{6,5},{7,6},{8,11},{9,8},{10,9... | collective-permute-start | bytes 589832 | tf_op jit(solution)/shard_map/ppermute | solution.py:506
  26.3 7.2 %shard_map.95 = (bf16[4,256,768]{2,1,0:T(8,128)(2,1)S(1)}, bf16[4,256,768]{2,1,0:T(8,128)(2,1)S(1)}) custom-call(s32[16]{0:T(128)S(1)} %stack.46.table_ref, bf16[64,1536]{1,0:T(8,128)(2,1)S(1)} %copy-done.1, bf16[64,1536]{1,0:T(8,128)(2,1)S(1)} %collective-permute-done.refs_1_.refs_5_, bf16[64,1536]{1,0:T(8,128)(2,1)S(1)} %collective-permute-done.1.refs_2_.refs_6_, ...), custom_call_target="tpu_custom_call" | custom-call | flops 4831838 | bytes 22806 | tf_op jit(solution)/shard_map/pallas_call | solution.py:317
  35.3 3.4 %collective-permute-done.5.got_ref = bf16[4,256,768]{2,1,0:T(8,128)(2,1)S(1)} collective-permute-done((bf16[4,256,768]{2,1,0:T(8,128)(2,1)S(1)}, bf16[4,256,768]{2,1,0:T(8,128)(2,1)S(1)}, u32[]{:S(2)}, u32[]{:S(2)}) %collective-permute-start.5) | collective-permute-done | bytes 1572896 | tf_op jit(solution)/shard_map/ppermute | solution.py:496
  42.5 6.6 %collective-permute-done.7.refs_2_.refs_3_.refs_4_ = bf16[64,1536]{1,0:T(8,128)(2,1)S(1)} collective-permute-done((bf16[64,1536]{1,0:T(8,128)(2,1)S(1)}, bf16[64,1536]{1,0:T(8,128)(2,1)S(1)}, u32[]{:S(2)}, u32[]{:S(2)}) %collective-permute-start.7) | collective-permute-done | bytes 196640 | tf_op jit(solution)/shard_map/ppermute | solution.py:509
  49.1 1.9 %collective-permute-done.6.near_ref = bf16[2,256,768]{2,1,0:T(8,128)(2,1)S(1)} collective-permute-done((bf16[2,256,768]{2,1,0:T(8,128)(2,1)S(1)}, bf16[2,256,768]{2,1,0:T(8,128)(2,1)S(1)}, u32[]{:S(2)}, u32[]{:S(2)}) %collective-permute-start.6) | collective-permute-done | bytes 786464 | tf_op jit(solution)/shard_map/ppermute | solution.py:499
  52.8 7.5 %shard_map.98 = (bf16[4,256,768]{2,1,0:T(8,128)(2,1)S(1)}, bf16[4,256,768]{2,1,0:T(8,128)(2,1)S(1)}) custom-call(s32[16]{0:T(128)S(1)} %stack.46.table_ref, bf16[64,1536]{1,0:T(8,128)(2,1)S(1)} %copy-done, bf16[64,1536]{1,0:T(8,128)(2,1)S(1)} %collective-permute-done.3.refs_1_.refs_2_.refs_3_, ...), custom_call_target="tpu_custom_call" | custom-call | flops 4831838 | bytes 22806 | tf_op jit(solution)/shard_map/pallas_call | solution.py:317
  65.6 2.9 %collective-permute-done.12.right_ref = bf16[256,768]{1,0:T(8,128)(2,1)S(1)} collective-permute-done((bf16[256,768]{1,0:T(8,128)(2,1)S(1)}, bf16[256,768]{1,0:T(8,128)(2,1)S(1)}, u32[]{:S(2)}, u32[]{:S(2)}) %collective-permute-start.12) | collective-permute-done | bytes 393248 | tf_op jit(solution)/shard_map/ppermute | solution.py:499
  69.2 3.7 %shard_map.102.refs_7_ = bf16[6144,1536]{1,0:T(8,128)(2,1)} custom-call(s32[16]{0:T(128)S(1)} %stack.46.table_ref, bf16[2,256,768]{2,1,0:T(8,128)(2,1)S(1)} %shard_map.101.refs_0_, bf16[64,1536]{1,0:T(8,128)(2,1)S(1)} %copy-done, bf16[64,1536]{1,0:T(8,128)(2,1)S(1)} %collective-permute-done.3.refs_1_.refs_2_.refs_3_, ...), custom_call_target="tpu_custom_call" | custom-call | flops 1207959 | bytes 5505 | tf_op jit(solution)/shard_map/pallas_call | solution.py:484
  73.0 9.1 %collective-permute-done.11.near_ref = bf16[2,256,768]{2,1,0:T(8,128)(2,1)S(1)} collective-permute-done((bf16[2,256,768]{2,1,0:T(8,128)(2,1)S(1)}, bf16[2,256,768]{2,1,0:T(8,128)(2,1)S(1)}, u32[]{:S(2)}, u32[]{:S(2)}) %collective-permute-start.11) | collective-permute-done | bytes 786464 | tf_op jit(solution)/shard_map/ppermute | solution.py:499
  82.8 4.0 %shard_map.104.refs_8_ = f32[256,1536]{1,0:T(8,128)S(1)} custom-call(s32[16]{0:T(128)S(1)} %stack.46.table_ref, bf16[2,256,768]{2,1,0:T(8,128)(2,1)S(1)} %shard_map.101.refs_0_, bf16[2,256,768]{2,1,0:T(8,128)(2,1)S(1)} %collective-permute-done.14.refs_1_.refs_0_, bf16[8,768,256]{2,1,0:T(8,128)(2,1)S(1)} %get-tuple-element.120.refs_5_.refs_2_, ...), custom_call_target="tpu_custom_call" | custom-call | flops 2415919 | bytes 12582 | tf_op jit(solution)/shard_map/pallas_call | solution.py:400
  86.8 3.7 %shard_map.105.refs_8_ = bf16[6144,1536]{1,0:T(8,128)(2,1)} custom-call(s32[16]{0:T(128)S(1)} %stack.46.table_ref, bf16[2,256,768]{2,1,0:T(8,128)(2,1)S(1)} %collective-permute-done.14.refs_1_.refs_0_, bf16[64,1536]{1,0:T(8,128)(2,1)S(1)} %copy-done, ...), custom_call_target="tpu_custom_call", output_to_operand_aliasing={{}: (8, {})} | custom-call | flops 1207959 | bytes 5505 | tf_op jit(solution)/shard_map/pallas_call | solution.py:484
  92.9 4.1 %shard_map.107 = (bf16[64,1536]{1,0:T(8,128)(2,1)S(1)}, bf16[64,1536]{1,0:T(8,128)(2,1)S(1)}, bf16[64,1536]{1,0:T(8,128)(2,1)S(1)}, bf16[64,1536]{1,0:T(8,128)(2,1)S(1)}) custom-call(s32[16]{0:T(128)S(1)} %stack.46.table_ref, bf16[2,256,768]{2,1,0:T(8,128)(2,1)S(1)} %collective-permute-done.16.refs_0_, ...), custom_call_target="tpu_custom_call" | custom-call | flops 2415919 | bytes 12582 | tf_op jit(solution)/shard_map/pallas_call | solution.py:400
  97.0 2.1 %collective-permute-done.15.right_ref = bf16[256,768]{1,0:T(8,128)(2,1)S(1)} collective-permute-done((bf16[256,768]{1,0:T(8,128)(2,1)S(1)}, bf16[256,768]{1,0:T(8,128)(2,1)S(1)}, u32[]{:S(2)}, u32[]{:S(2)}) %collective-permute-start.15) | collective-permute-done | bytes 393248 | tf_op jit(solution)/shard_map/ppermute | solution.py:499
  101.4 3.9 %collective-permute-start.19 = (bf16[64,1536]{1,0:T(8,128)(2,1)S(1)}, bf16[64,1536]{1,0:T(8,128)(2,1)S(1)}, u32[]{:S(2)}, u32[]{:S(2)}) collective-permute-start(bf16[64,1536]{1,0:T(8,128)(2,1)S(1)} %get-tuple-element.175), channel_id=1, source_target_pairs={{0,1},{1,2},{4,5},{5,6},{8,9},{9,10},{12,13},{13,14},{16,17},{17,1... | collective-permute-start | bytes 589832 | tf_op jit(solution)/shard_map/ppermute | solution.py:509
  105.4 4.2 %shard_map.109.refs_7_ = f32[256,1536]{1,0:T(8,128)S(1)} custom-call(s32[16]{0:T(128)S(1)} %stack.46.table_ref, bf16[2,256,768]{2,1,0:T(8,128)(2,1)S(1)} %shard_map.108.refs_0_, bf16[2,256,768]{2,1,0:T(8,128)(2,1)S(1)} %collective-permute-done.21.refs_1_, bf16[8,256,768]{2,1,0:T(8,128)(2,1)S(1)} %get-tuple-element.122.refs_4_.refs_2_.refs_1_, ...), custom_call_target="tpu_custom_call" | custom-call | flops 2415919 | bytes 12582 | tf_op jit(solution)/shard_map/pallas_call | solution.py:400
  112.7 2.4 %collective-permute-start.23 = (bf16[64,1536]{1,0:T(8,128)(2,1)S(1)}, bf16[64,1536]{1,0:T(8,128)(2,1)S(1)}, u32[]{:S(2)}, u32[]{:S(2)}) collective-permute-start(bf16[64,1536]{1,0:T(8,128)(2,1)S(1)} %get-tuple-element.184), channel_id=1, source_target_pairs={{0,3},{1,0},{2,1},{3,2},{4,7},{5,4},{6,5},{7,6},{8,11},{9,8},{10,9... | collective-permute-start | bytes 589832 | tf_op jit(solution)/shard_map/ppermute | solution.py:506
  115.1 2.4 %shard_map.111.refs_7_ = f32[256,1536]{1,0:T(8,128)S(1)} custom-call(s32[16]{0:T(128)S(1)} %stack.46.table_ref, bf16[2,256,768]{2,1,0:T(8,128)(2,1)S(1)} %collective-permute-done.18.refs_0_.refs_2_, bf16[8,256,768]{2,1,0:T(8,128)(2,1)S(1)} %get-tuple-element.122.refs_4_.refs_2_.refs_1_, bf16[8,256,768]{2,1,0:T(8,128)(2,1)S(1)} %get-tuple-element.123.refs_5_.refs_3_.refs_2_, ...), custom_call_target="tpu_custom_call" | custom-call | flops 1207959 | bytes 7077 | tf_op jit(solution)/shard_map/pallas_call | solution.py:400
  117.5 2.5 %shard_map.112 = (bf16[64,1536]{1,0:T(8,128)(2,1)S(1)}, bf16[64,1536]{1,0:T(8,128)(2,1)S(1)}, bf16[64,1536]{1,0:T(8,128)(2,1)S(1)}, bf16[64,1536]{1,0:T(8,128)(2,1)S(1)}) custom-call(s32[16]{0:T(128)S(1)} %stack.46.table_ref, bf16[2,256,768]{2,1,0:T(8,128)(2,1)S(1)} %collective-permute-done.24.refs_0_.refs_3_, ...), custom_call_target="tpu_custom_call" | custom-call | flops 1207959 | bytes 7077 | tf_op jit(solution)/shard_map/pallas_call | solution.py:400
  121.4 1.9 %collective-permute-start.27 = (bf16[64,1536]{1,0:T(8,128)(2,1)S(1)}, bf16[64,1536]{1,0:T(8,128)(2,1)S(1)}, u32[]{:S(2)}, u32[]{:S(2)}) collective-permute-start(bf16[64,1536]{1,0:T(8,128)(2,1)S(1)} %get-tuple-element.195), channel_id=1, source_target_pairs={{0,1},{1,2},{2,3},{3,0},{4,5},{5,6},{6,7},{7,4},{8,9},{9,10},{10,1... | collective-permute-start | bytes 589832 | tf_op jit(solution)/shard_map/ppermute | solution.py:506
  123.3 6.0 %shard_map.113 = bf16[6144,1536]{1,0:T(8,128)(2,1)} custom-call(s32[16]{0:T(128)S(1)} %stack.46.table_ref, bf16[2,256,768]{2,1,0:T(8,128)(2,1)S(1)} %collective-permute-done.16.refs_0_, bf16[2,256,768]{2,1,0:T(8,128)(2,1)S(1)} %collective-permute-done.17.refs_1_, bf16[64,1536]{1,0:T(8,128)(2,1)S(1)} %copy-done, ...), custom_call_target="tpu_custom_call", output_to_operand_aliasing={{}: (9, {})} | custom-call | flops 2415919 | bytes 11010 | tf_op jit(solution)/shard_map/pallas_call | solution.py:484
  129.4 10.7 %shard_map.114 = bf16[1536,6144]{1,0:T(8,128)(2,1)} custom-call(s32[16]{0:T(128)S(1)} %stack.46.table_ref, bf16[2,256,768]{2,1,0:T(8,128)(2,1)S(1)} %shard_map.108.refs_0_, bf16[2,256,768]{2,1,0:T(8,128)(2,1)S(1)} %collective-permute-done.21.refs_1_, bf16[2,256,768]{2,1,0:T(8,128)(2,1)S(1)} %collective-permute-done.18.refs_0_.refs_2_, ...), custom_call_target="tpu_custom_call" | custom-call | flops 4831838 | bytes 22020 | tf_op jit(solution)/shard_map/pallas_call | solution.py:484
  (69 shorter events, 28.7 us)
Async XLA Ops:
  0.6 22.8 %collective-permute-start.2 = (bf16[64,1536]{1,0:T(8,128)(2,1)}, bf16[64,1536]{1,0:T(8,128)(2,1)S(1)}, u32[]{:S(2)}, u32[]{:S(2)}) collective-permute-start(bf16[64,1536]{1,0:T(8,128)(2,1)} %refs_4_.1), channel_id=1, source_target_pairs={{0,3},{1,0},{2,1},{3,2},{4,7},{5,4},{6,5},{7,6},{8,11},{9,8},{10,9... | collective-permute-start | bytes 589832 | tf_op jit(solution)/shard_map/ppermute | solution.py:506
  5.7 17.7 %collective-permute-start.1 = (bf16[64,1536]{1,0:T(8,128)(2,1)}, bf16[64,1536]{1,0:T(8,128)(2,1)S(1)}, u32[]{:S(2)}, u32[]{:S(2)}) collective-permute-start(bf16[64,1536]{1,0:T(8,128)(2,1)} %refs_4_.1), channel_id=1, source_target_pairs={{0,2},{1,3},{2,0},{3,1},{4,6},{5,7},{6,4},{7,5},{8,10},{9,11},{10,... | collective-permute-start | bytes 589832 | tf_op jit(solution)/shard_map/ppermute | solution.py:506
  5.7 17.7 %collective-permute-start = (bf16[64,1536]{1,0:T(8,128)(2,1)}, bf16[64,1536]{1,0:T(8,128)(2,1)S(1)}, u32[]{:S(2)}, u32[]{:S(2)}) collective-permute-start(bf16[64,1536]{1,0:T(8,128)(2,1)} %refs_4_.1), channel_id=1, source_target_pairs={{0,1},{1,2},{2,3},{3,0},{4,5},{5,6},{6,7},{7,4},{8,9},{9,10},{10,1... | collective-permute-start | bytes 589832 | tf_op jit(solution)/shard_map/ppermute | solution.py:506
  23.5 10.1 %collective-permute-start.4 = (bf16[64,1536]{1,0:T(8,128)(2,1)S(1)}, bf16[64,1536]{1,0:T(8,128)(2,1)S(1)}, u32[]{:S(2)}, u32[]{:S(2)}) collective-permute-start(bf16[64,1536]{1,0:T(8,128)(2,1)S(1)} %copy-done), channel_id=1, source_target_pairs={{0,3},{1,0},{2,1},{3,2},{4,7},{5,4},{6,5},{7,6},{8,11},{9,8},{10,9... | collective-permute-start | bytes 589832 | tf_op jit(solution)/shard_map/ppermute | solution.py:506
  26.3 8.9 %collective-permute-start.3 = (bf16[64,1536]{1,0:T(8,128)(2,1)S(1)}, bf16[64,1536]{1,0:T(8,128)(2,1)S(1)}, u32[]{:S(2)}, u32[]{:S(2)}) collective-permute-start(bf16[64,1536]{1,0:T(8,128)(2,1)S(1)} %copy-done), channel_id=1, source_target_pairs={{0,1},{1,2},{2,3},{3,0},{4,5},{5,6},{6,7},{7,4},{8,9},{9,10},{10,1... | collective-permute-start | bytes 589832 | tf_op jit(solution)/shard_map/ppermute | solution.py:506
  39.0 12.1 %collective-permute-start.6 = (bf16[2,256,768]{2,1,0:T(8,128)(2,1)S(1)}, bf16[2,256,768]{2,1,0:T(8,128)(2,1)S(1)}, u32[]{:S(2)}, u32[]{:S(2)}) collective-permute-start(bf16[2,256,768]{2,1,0:T(8,128)(2,1)S(1)} %get-tuple-element.133), channel_id=1, source_target_pairs={{0,8},{4,20},{8,0},{12,28},{16,24},{20,4},{24,16},{28,12},{1,9},{5... | collective-permute-start | bytes 2359304 | tf_op jit(solution)/shard_map/ppermute | solution.py:499
  40.6 8.6 %collective-permute-start.7 = (bf16[64,1536]{1,0:T(8,128)(2,1)S(1)}, bf16[64,1536]{1,0:T(8,128)(2,1)S(1)}, u32[]{:S(2)}, u32[]{:S(2)}) collective-permute-start(bf16[64,1536]{1,0:T(8,128)(2,1)S(1)} %collective-permute-done.4.refs_4_.refs_5_.refs_6_), channel_id=1, source_target_pairs={{1,0},{2,1},{5,4},{6,5},{9,8},{10,9},{13,12},{14,13},{17,16},{18,1... | collective-permute-start | bytes 589832 | tf_op jit(solution)/shard_map/ppermute | solution.py:509
  41.8 7.3 %collective-permute-start.8 = (bf16[64,1536]{1,0:T(8,128)(2,1)S(1)}, bf16[64,1536]{1,0:T(8,128)(2,1)S(1)}, u32[]{:S(2)}, u32[]{:S(2)}) collective-permute-start(bf16[64,1536]{1,0:T(8,128)(2,1)S(1)} %collective-permute-done.3.refs_1_.refs_2_.refs_3_), channel_id=1, source_target_pairs={{1,2},{2,3},{5,6},{6,7},{9,10},{10,11},{13,14},{14,15},{17,18},{18... | collective-permute-start | bytes 589832 | tf_op jit(solution)/shard_map/ppermute | solution.py:509
  51.2 9.1 %collective-permute-start.9 = (bf16[256,768]{1,0:T(8,128)(2,1)S(1)}, bf16[256,768]{1,0:T(8,128)(2,1)S(1)}, u32[]{:S(2)}, u32[]{:S(2)}) collective-permute-start(bf16[256,768]{1,0:T(8,128)(2,1)S(1)} %get-tuple-element.138), channel_id=1, source_target_pairs={{0,16},{4,12},{8,24},{12,4},{16,0},{20,28},{24,8},{28,20},{1,17},{... | collective-permute-start | bytes 1179656 | tf_op jit(solution)/shard_map/ppermute | solution.py:503
  60.7 7.8 %collective-permute-start.12 = (bf16[256,768]{1,0:T(8,128)(2,1)S(1)}, bf16[256,768]{1,0:T(8,128)(2,1)S(1)}, u32[]{:S(2)}, u32[]{:S(2)}) collective-permute-start(bf16[256,768]{1,0:T(8,128)(2,1)S(1)} %get-tuple-element.152.left_ref), channel_id=1, source_target_pairs={{0,8},{4,20},{8,0},{12,28},{16,24},{20,4},{24,16},{28,12},{1,9},{5... | collective-permute-start | bytes 1179656 | tf_op jit(solution)/shard_map/ppermute | solution.py:499
  64.1 18.0 %collective-permute-start.11 = (bf16[2,256,768]{2,1,0:T(8,128)(2,1)S(1)}, bf16[2,256,768]{2,1,0:T(8,128)(2,1)S(1)}, u32[]{:S(2)}, u32[]{:S(2)}) collective-permute-start(bf16[2,256,768]{2,1,0:T(8,128)(2,1)S(1)} %get-tuple-element.156), channel_id=1, source_target_pairs={{0,8},{4,20},{8,0},{12,28},{16,24},{20,4},{24,16},{28,12},{1,9},{5... | collective-permute-start | bytes 2359304 | tf_op jit(solution)/shard_map/ppermute | solution.py:499
  68.6 14.2 %collective-permute-start.14 = (bf16[2,256,768]{2,1,0:T(8,128)(2,1)S(1)}, bf16[2,256,768]{2,1,0:T(8,128)(2,1)S(1)}, u32[]{:S(2)}, u32[]{:S(2)}) collective-permute-start(bf16[2,256,768]{2,1,0:T(8,128)(2,1)S(1)} %shard_map.101.refs_0_), channel_id=1, source_target_pairs={{0,4},{4,0},{8,12},{12,8},{16,20},{20,16},{24,28},{28,24},{1,5},{5... | collective-permute-start | bytes 2359304 | tf_op jit(solution)/shard_map/ppermute | solution.py:496
  68.7 21.9 %collective-permute-start.16 = (bf16[2,256,768]{2,1,0:T(8,128)(2,1)S(1)}, bf16[2,256,768]{2,1,0:T(8,128)(2,1)S(1)}, u32[]{:S(2)}, u32[]{:S(2)}) collective-permute-start(bf16[2,256,768]{2,1,0:T(8,128)(2,1)S(1)} %shard_map.101.refs_0_), channel_id=1, source_target_pairs={{0,16},{4,12},{8,24},{12,4},{16,0},{20,28},{24,8},{28,20},{1,17},{... | collective-permute-start | bytes 2359304 | tf_op jit(solution)/shard_map/ppermute | solution.py:503
  82.2 8.3 %collective-permute-start.13 = (bf16[256,768]{1,0:T(8,128)(2,1)S(1)}, bf16[256,768]{1,0:T(8,128)(2,1)S(1)}, u32[]{:S(2)}, u32[]{:S(2)}) collective-permute-start(bf16[256,768]{1,0:T(8,128)(2,1)S(1)} %get-tuple-element.161), channel_id=1, source_target_pairs={{0,16},{4,12},{8,24},{12,4},{16,0},{20,28},{24,8},{28,20},{1,17},{... | collective-permute-start | bytes 1179656 | tf_op jit(solution)/shard_map/ppermute | solution.py:503
  91.2 7.8 %collective-permute-start.15 = (bf16[256,768]{1,0:T(8,128)(2,1)S(1)}, bf16[256,768]{1,0:T(8,128)(2,1)S(1)}, u32[]{:S(2)}, u32[]{:S(2)}) collective-permute-start(bf16[256,768]{1,0:T(8,128)(2,1)S(1)} %shard_map.106.left_ref), channel_id=1, source_target_pairs={{0,8},{4,20},{8,0},{12,28},{16,24},{20,4},{24,16},{28,12},{1,9},{5... | collective-permute-start | bytes 1179656 | tf_op jit(solution)/shard_map/ppermute | solution.py:499
  99.1 6.3 %collective-permute-start.21 = (bf16[2,256,768]{2,1,0:T(8,128)(2,1)S(1)}, bf16[2,256,768]{2,1,0:T(8,128)(2,1)S(1)}, u32[]{:S(2)}, u32[]{:S(2)}) collective-permute-start(bf16[2,256,768]{2,1,0:T(8,128)(2,1)S(1)} %shard_map.108.refs_0_), channel_id=1, source_target_pairs={{0,4},{4,0},{8,12},{12,8},{16,20},{20,16},{24,28},{28,24},{1,5},{5... | collective-permute-start | bytes 2359304 | tf_op jit(solution)/shard_map/ppermute | solution.py:496
  99.2 12.1 %collective-permute-start.18 = (bf16[2,256,768]{2,1,0:T(8,128)(2,1)S(1)}, bf16[2,256,768]{2,1,0:T(8,128)(2,1)S(1)}, u32[]{:S(2)}, u32[]{:S(2)}) collective-permute-start(bf16[2,256,768]{2,1,0:T(8,128)(2,1)S(1)} %shard_map.108.refs_0_), channel_id=1, source_target_pairs={{0,16},{4,12},{8,24},{12,4},{16,0},{20,28},{24,8},{28,20},{1,17},{... | collective-permute-start | bytes 2359304 | tf_op jit(solution)/shard_map/ppermute | solution.py:503
  100.8 8.8 %collective-permute-start.20 = (bf16[64,1536]{1,0:T(8,128)(2,1)S(1)}, bf16[64,1536]{1,0:T(8,128)(2,1)S(1)}, u32[]{:S(2)}, u32[]{:S(2)}) collective-permute-start(bf16[64,1536]{1,0:T(8,128)(2,1)S(1)} %get-tuple-element.175), channel_id=1, source_target_pairs={{2,1},{3,2},{6,5},{7,6},{10,9},{11,10},{14,13},{15,14},{18,17},{19... | collective-permute-start | bytes 589832 | tf_op jit(solution)/shard_map/ppermute | solution.py:509
  101.4 8.4 %collective-permute-start.19 = (bf16[64,1536]{1,0:T(8,128)(2,1)S(1)}, bf16[64,1536]{1,0:T(8,128)(2,1)S(1)}, u32[]{:S(2)}, u32[]{:S(2)}) collective-permute-start(bf16[64,1536]{1,0:T(8,128)(2,1)S(1)} %get-tuple-element.175), channel_id=1, source_target_pairs={{0,1},{1,2},{4,5},{5,6},{8,9},{9,10},{12,13},{13,14},{16,17},{17,1... | collective-permute-start | bytes 589832 | tf_op jit(solution)/shard_map/ppermute | solution.py:509
  111.3 28.8 %collective-permute-start.22 = (bf16[64,1536]{1,0:T(8,128)(2,1)S(1)}, bf16[64,1536]{1,0:T(8,128)(2,1)S(1)}, u32[]{:S(2)}, u32[]{:S(2)}) collective-permute-start(bf16[64,1536]{1,0:T(8,128)(2,1)S(1)} %get-tuple-element.183), channel_id=1, source_target_pairs={{0,1},{1,2},{2,3},{3,0},{4,5},{5,6},{6,7},{7,4},{8,9},{9,10},{10,1... | collective-permute-start | bytes 589832 | tf_op jit(solution)/shard_map/ppermute | solution.py:506
  112.7 27.4 %collective-permute-start.23 = (bf16[64,1536]{1,0:T(8,128)(2,1)S(1)}, bf16[64,1536]{1,0:T(8,128)(2,1)S(1)}, u32[]{:S(2)}, u32[]{:S(2)}) collective-permute-start(bf16[64,1536]{1,0:T(8,128)(2,1)S(1)} %get-tuple-element.184), channel_id=1, source_target_pairs={{0,3},{1,0},{2,1},{3,2},{4,7},{5,4},{6,5},{7,6},{8,11},{9,8},{10,9... | collective-permute-start | bytes 589832 | tf_op jit(solution)/shard_map/ppermute | solution.py:506
  120.0 20.8 %collective-permute-start.25 = (bf16[64,1536]{1,0:T(8,128)(2,1)S(1)}, bf16[64,1536]{1,0:T(8,128)(2,1)S(1)}, u32[]{:S(2)}, u32[]{:S(2)}) collective-permute-start(bf16[64,1536]{1,0:T(8,128)(2,1)S(1)} %get-tuple-element.193), channel_id=1, source_target_pairs={{0,3},{1,0},{2,1},{3,2},{4,7},{5,4},{6,5},{7,6},{8,11},{9,8},{10,9... | collective-permute-start | bytes 589832 | tf_op jit(solution)/shard_map/ppermute | solution.py:506
  121.0 20.4 %collective-permute-start.26 = (bf16[64,1536]{1,0:T(8,128)(2,1)S(1)}, bf16[64,1536]{1,0:T(8,128)(2,1)S(1)}, u32[]{:S(2)}, u32[]{:S(2)}) collective-permute-start(bf16[64,1536]{1,0:T(8,128)(2,1)S(1)} %get-tuple-element.194), channel_id=1, source_target_pairs={{0,2},{1,3},{2,0},{3,1},{4,6},{5,7},{6,4},{7,5},{8,10},{9,11},{10,... | collective-permute-start | bytes 589832 | tf_op jit(solution)/shard_map/ppermute | solution.py:506
  121.4 20.0 %collective-permute-start.27 = (bf16[64,1536]{1,0:T(8,128)(2,1)S(1)}, bf16[64,1536]{1,0:T(8,128)(2,1)S(1)}, u32[]{:S(2)}, u32[]{:S(2)}) collective-permute-start(bf16[64,1536]{1,0:T(8,128)(2,1)S(1)} %get-tuple-element.195), channel_id=1, source_target_pairs={{0,1},{1,2},{2,3},{3,0},{4,5},{5,6},{6,7},{7,4},{8,9},{9,10},{10,1... | collective-permute-start | bytes 589832 | tf_op jit(solution)/shard_map/ppermute | solution.py:506
  (6 other events, 33.0 us)

commit v2 on v1

--- a/solution.py
+++ b/solution.py
@@ -9,6 +9,7 @@
 
 TILE = 128
 VMEM_LIMIT = 11 << 20
+TAIL_LIMIT = 24 << 20
 PIECE = 256
 F32 = jnp.float32
 BF16 = jnp.bfloat16
@@ -80,7 +81,7 @@
 
 
 AT_SENT, AT_HELD, AT_NEAR, AT_FAR = 0, 4, 8, 12
-AT_NEAR_CORE, AT_FAR_CORE = 10, 14
+AT_NEAR_CORE = 10
 
 
 def spans(length):
@@ -208,16 +209,18 @@
     return small(body, [(left.shape, BF16) for left, _ in pairs], *flat(pairs))
 
 
-def added(terms):
+def added(*sums):
     def body(*refs):
-        *given, out = refs
-        out[...] = functools.reduce(jnp.add, [ref[...].astype(F32) for ref in given]).astype(BF16)
+        refs, outs = iter(refs[: -len(sums)]), refs[-len(sums) :]
+        for terms, out in zip(sums, outs):
+            values = [next(refs)[...].astype(F32) for _ in terms]
+            out[...] = functools.reduce(jnp.add, values).astype(BF16)
 
     return pl.pallas_call(
         body,
-        out_shape=jax.ShapeDtypeStruct(terms[0].shape, BF16),
+        out_shape=tuple(jax.ShapeDtypeStruct(terms[0].shape, BF16) for terms in sums),
         compiler_params=pltpu.CompilerParams(vmem_limit_bytes=VMEM_LIMIT),
-    )(*terms)
+    )(*flat(sums))
 
 
 def kept_pieces(weight, keep, shares, by_rows, pieces):
@@ -317,13 +320,13 @@
     return call(table, *flat(parts), *map(in_vmem, kept))
 
 
-def fetch(i, pairs, refs, held, sems):
+def fetch(i, pairs, refs, held, sems, begin):
     copies = [
         pltpu.make_async_copy(ref, held.at[pl.ds(2 * n, 2)], sems.at[n])
         for n, ref in enumerate(refs)
     ]
 
-    @pl.when(i == 0)
+    @pl.when(begin)
     def _():
         for copy in copies:
             copy.start()
@@ -351,7 +354,7 @@
         else:
             total, held, sems = refs
         i = pl.program_id(0)
-        fetch(i, pairs, pair_refs, held, sems)
+        fetch(i, pairs, pair_refs, held, sems, i == 0)
 
         @pl.when(i == 0)
         def _():
@@ -400,88 +403,127 @@
     return call(table, *pairs, *map(in_vmem, kept), *given)
 
 
-def weight_gradient(table, at, pairs, parts, keep, shape, by_rows, into=None):
-    tokens = sum(part[0].shape[0] for part in parts)
-    share = pairs[0].shape[2]
-    wide = parts[0][0].shape[1]
-    count = len(flat(parts))
-    steps = 2 * len(pairs)
-    block = (share, wide) if by_rows else (wide, share)
-    given = [] if into is None else [into]
-
-    def body(table_ref, *refs):
-        pair_refs, refs = refs[: len(pairs)], refs[len(pairs) :]
-        part_refs, refs = refs[:count], refs[count:]
-        keep_ref, *_, out, made, held, other, sems, out_sems = refs
-        i = pl.program_id(0)
-        slot = i % 2
-
-        def copy(step):
-            start = pl.multiple_of(table_ref[at + step] * share, TILE)
-            if by_rows:
-                target = out.at[pl.ds(start, share)]
-            else:
-                target = out.at[:, pl.ds(start, share)]
-            return pltpu.make_async_copy(made.at[step % 2], target, out_sems.at[step % 2])
+class Gradient:
+
+    def __init__(self, at, pairs, parts, keep, shape, by_rows, into=None):
+        self.at, self.pairs, self.parts, self.keep = at, pairs, parts, keep
+        self.shape, self.by_rows = shape, by_rows
+        self.given = [] if into is None else [into]
+        self.arrays = [*pairs, *flat(parts), keep, *self.given]
+        self.steps = 2 * len(pairs)
+        self.tokens, self.share = pairs[0].shape[1:]
+        self.wide = parts[0][0].shape[1]
+        sides = (self.share, self.wide)
+        self.block = sides if by_rows else sides[::-1]
+
+    def specs(self, first):
+        anywhere = pl.BlockSpec(memory_space=pl.ANY)
+
+        def place(i, t):
+            return t[self.at + jnp.clip(i - first, 0, self.steps - 1)], 0, 0
+
+        return (
+            [anywhere] * len(self.pairs)
+            + [whole(array) for array in flat(self.parts)]
+            + [pl.BlockSpec((None,) + self.keep.shape[1:], place)]
+            + [anywhere] * len(self.given)
+        )
+
+    def scratch(self):
+        other = (self.tokens, self.wide) if self.by_rows else (self.wide, self.tokens)
+        return [
+            pltpu.VMEM((2,) + self.block, BF16),
+            pltpu.VMEM((self.steps, self.tokens, self.share), BF16),
+            pltpu.VMEM(other, BF16),
+            pltpu.SemaphoreType.DMA((len(self.pairs),)),
+            pltpu.SemaphoreType.DMA((2,)),
+        ]
+
+    def copy(self, table_ref, out, made, out_sems, step):
+        start = pl.multiple_of(table_ref[self.at + step] * self.share, TILE)
+        target = out.at[pl.ds(start, self.share)] if self.by_rows else out.at[:, pl.ds(start, self.share)]
+        return pltpu.make_async_copy(made.at[step % 2], target, out_sems.at[step % 2])
+
+    def run(self, table_ref, refs, out, scratch, i, begin):
+        count = len(self.pairs)
+        pair_refs, refs = refs[:count], refs[count:]
+        count = len(flat(self.parts))
+        part_refs, keep_ref = refs[:count], refs[count]
+        made, held, other, sems, out_sems = scratch
+        fetch(i, self.pairs, pair_refs, held, sems, begin)
 
         @pl.when(i == 0)
         def _():
-            values = parts_of(part_refs, parts)
-            if by_rows:
+            values = parts_of(part_refs, self.parts)
+            if self.by_rows:
                 stack(other, values)
             else:
                 other[...] = jnp.concatenate(values).T
 
-        fetch(i, pairs, pair_refs, held, sems)
-
-        @pl.when(i >= 2)
+        @pl.when((i >= 2) & (i < self.steps))
         def _():
-            copy(i - 2).wait()
-
-        left = held[i].T if by_rows else other
-        right = other if by_rows else held.at[i]
-        span = share if block[0] % share == 0 else TILE
-        for lo in range(0, block[0], span):
-            for columns in spans(block[1]):
-                term = contract(left[lo : lo + span, :], right[:, columns], 1, 0)
-                for k in range(0, span, TILE):
-                    tile = (lo + k) // TILE
-                    made[slot, lo + k : lo + k + TILE, columns] = (
-                        term[k : k + TILE].astype(BF16) * keep_ref[tile : tile + 1, columns]
-                    )
-        copy(i).start()
+            self.copy(table_ref, out, made, out_sems, i - 2).wait()
+
+        @pl.when((i >= 0) & (i < self.steps))
+        def _():
+            left = held[i].T if self.by_rows else other
+            right = other if self.by_rows else held.at[i]
+            for lo in range(0, self.block[0], self.share):
+                for columns in spans(self.block[1]):
+                    term = contract(left[lo : lo + self.share, :], right[:, columns], 1, 0)
+                    for k in range(0, self.share, TILE):
+                        row = lo + k
+                        tile = row // TILE
+                        made[i % 2, row : row + TILE, columns] = (
+                            term[k : k + TILE].astype(BF16) * keep_ref[tile : tile + 1, columns]
+                        )
+            self.copy(table_ref, out, made, out_sems, i).start()
+
+
+def weight_gradients(table, jobs, limit=VMEM_LIMIT):
+    firsts = [sum(job.steps for job in jobs[:n]) for n in range(len(jobs))]
+    steps = sum(job.steps for job in jobs)
+
+    def body(table_ref, *refs):
+        refs = list(refs)
+        operands = [[refs.pop(0) for _ in job.arrays] for job in jobs]
+        outs = [refs.pop(0) for _ in jobs]
+        scratch = [[refs.pop(0) for _ in job.scratch()] for job in jobs]
+        i = pl.program_id(0)
+        for job, first, given, out, own in zip(jobs, firsts, operands, outs, scratch):
+            job.run(table_ref, given, out, own, i - first, i == 0)
 
         @pl.when(i == steps - 1)
         def _():
-            copy(i - 1).wait()
-            copy(i).wait()
-
-    call = pl.pallas_call(
+            for job, out, (made, *_, out_sems) in zip(jobs, outs, scratch):
+                for step in (job.steps - 2, job.steps - 1):
+                    job.copy(table_ref, out, made, out_sems, step).wait()
+
+    aliases, at = {}, 1
+    for n, job in enumerate(jobs):
+        at += len(job.arrays)
+        if job.given:
+            aliases[at - 1] = n
+    outs = pl.pallas_call(
         body,
-        out_shape=jax.ShapeDtypeStruct(shape, BF16),
+        out_shape=tuple(jax.ShapeDtypeStruct(job.shape, BF16) for job in jobs),
         grid_spec=pltpu.PrefetchScalarGridSpec(
             num_scalar_prefetch=1,
             grid=(steps,),
-            in_specs=[pl.BlockSpec(memory_space=pl.ANY)] * len(pairs)
-            + [whole(array) for array in flat(parts)]
-            + [pl.BlockSpec((None,) + keep.shape[1:], lambda i, t: (t[at + i], 0, 0))]
-            + [pl.BlockSpec(memory_space=pl.ANY)] * len(given),
-            out_specs=pl.BlockSpec(memory_space=pl.ANY),
-            scratch_shapes=[
-                pltpu.VMEM((2,) + block, BF16),
-                pltpu.VMEM((steps, tokens, share), BF16),
-                pltpu.VMEM((tokens, wide) if by_rows else (wide, tokens), BF16),
-                pltpu.SemaphoreType.DMA((len(pairs),)),
-                pltpu.SemaphoreType.DMA((2,)),
-            ],
+            in_specs=flat([job.specs(first) for job, first in zip(jobs, firsts)]),
+            out_specs=(pl.BlockSpec(memory_space=pl.ANY),) * len(jobs),
+            scratch_shapes=flat([job.scratch() for job in jobs]),
         ),
-        input_output_aliases={2 + len(pairs) + count: 0} if given else {},
-        compiler_params=params(),
+        input_output_aliases=aliases,
+        compiler_params=pltpu.CompilerParams(
+            dimension_semantics=("arbitrary",), vmem_limit_bytes=limit
+        ),
         cost_estimate=cost(
-            2 * tokens * share * wide * steps, 2 * share * (wide + tokens) * steps
+            sum(2 * job.tokens * job.share * job.wide * job.steps for job in jobs),
+            sum(2 * job.share * (job.wide + job.tokens) * job.steps for job in jobs),
         ),
     )
-    return call(table, *pairs, *flat(parts), keep, *given)
+    return outs(table, *flat([job.arrays for job in jobs]))
 
 
 def per_device_tuned(n_row, n_col, inputs, w_up, w_down, mask_up, mask_down, cotangent):
@@ -556,10 +598,11 @@
     act_far = along_second(act_near)
     act_core = between_cores(act_near)
 
-    def grad_down_of(start, at, pairs, into=None):
-        return weight_gradient(
-            after(table, start), at, pairs, cot_all, keep_down, w_down.shape, True, into
-        )
+    def grad_down_job(at, pairs, into=None):
+        return Gradient(at, pairs, cot_all, keep_down, w_down.shape, True, into)
+
+    def grad_down_of(start, *job):
+        return weight_gradients(after(table, start), [grad_down_job(*job)])[0]
 
     grad_down = grad_down_of(act_near, AT_NEAR, [act_near])
     near, grad_down = together(near, grad_down)
@@ -590,23 +633,28 @@
     )
     out_terms = [out_blocks[0], along_col(to_upper, 1), along_col(to_lower, -1)]
     grad_far_core = between_cores(grad_far)
-    in_total = gathered(table, AT_FAR, [grad_far], up, False, in_total)
-    in_blocks = gathered(table, AT_FAR_CORE, [grad_far_core], up, False, in_total, n_col)
+    in_blocks = gathered(
+        table, AT_FAR, [grad_far, grad_far_core], up, False, in_total, n_col
+    )
 
     in_terms = col_sum(in_blocks)
-    grad_down = grad_down_of(in_blocks[0], AT_FAR, [act_far, act_far_core], grad_down)
-    grad_up = weight_gradient(
-        after(table, grad_down),
-        AT_NEAR,
-        [grad_near, grad_core, grad_far, grad_far_core],
-        inputs_all,
-        keep_up,
-        w_up.shape,
-        False,
+    grad_down, grad_up = weight_gradients(
+        after(table, in_blocks[0]),
+        [
+            grad_down_job(AT_FAR, [act_far, act_far_core], grad_down),
+            Gradient(
+                AT_NEAR,
+                [grad_near, grad_core, grad_far, grad_far_core],
+                inputs_all,
+                keep_up,
+                w_up.shape,
+                False,
+            ),
+        ],
+        TAIL_LIMIT,
     )
     out_terms[1:] = together(*out_terms[1:], grad_up)[:-1]
-    outputs = added(out_terms)
-    grad_inputs = added(in_terms)
+    outputs, grad_inputs = added(out_terms, in_terms)
     return (outputs, grad_inputs, grad_up, grad_down)
 
 

time: 143 us -> 143 us (level)
  Pallas kernels: 73.8 us -> 70.7 us
  waiting for transfers between devices: 31.6 us -> 34.6 us
    ppermute x10, waiting for transfers between devices: 2.34 us -> 5.37 us  [along_col(): lax.ppermute(value, 'col', [(i, (i + shift) % n_col) for i in range(n_col)])]
    pallas_call x6 -> x4, Pallas kernels: 25.7 us -> 23.2 us  [the longest x3 22.4 us: weight_gradients(): return outs(table, *flat([job.arrays for job in jobs]))]
    pallas_call x5 -> x4, Pallas kernels: 17.1 us -> 16.4 us  [gathered(): return call(table, *pairs, *map(in_vmem, kept), *given)]
  transfers between devices with their start and end apart: 28 -> 28, of which waited for: 12 -> 12; matrix products, arithmetic and copies ran while one was open for 2% -> 2% of each run, Pallas kernels for 51% -> 49%
where the time goes in v2:
time: 143 us; the launch traced here: 142 us
  Pallas kernels  70.7 us (49%)
  waiting for transfers between devices  34.6 us (24%)
  starting transfers between devices  33.7 us (24%)
    pallas_call x3, Pallas kernels, weight_gradients(): return outs(table, *flat([job.arrays for job in jobs]))  22.4 us
    pallas_call x4, Pallas kernels, gathered(): return call(table, *pairs, *map(in_vmem, kept), *given)  16.4 us
    ppermute x10, starting transfers between devices, along_col(): lax.ppermute(value, 'col', [(i, (i + shift) % n_col) for i in range(n_col)])  16.4 us
    ppermute x4, waiting for transfers between devices, along_first(): lax.ppermute(value, 'row', [(i, i ^ first_of(i)) for i in range(n_row)])  16 us
    pallas_call x2, Pallas kernels, project(): return call(table, *flat(parts), *map(in_vmem, kept))  14.7 us
    pallas_call x2, Pallas kernels, kept_pieces(): pl.pallas_call(body, out_shape=(pltpu.VMEM((shares,) + block, BF16),) * l...  14.3 us
    ppermute x4, waiting for transfers between devices, toward(): return lax.ppermute(value, 'col', [(i, i + step) for i in froms])  6.84 us
    ppermute x4, starting transfers between devices, toward(): return lax.ppermute(value, 'col', [(i, i + step) for i in froms])  6.55 us
  transfers between devices with their start and end apart: 28, of which 12 were waited for; matrix products, arithmetic and copies ran while one was open for 2% of the time, Pallas kernels for 49%

profile of v2, /device:TPU:0, one launch (start us, length us, event | category | flops | bytes accessed | tf_op | source)
XLA Modules:
  0.0 142.4 jit_solution(16939621733079928997)
XLA Ops:
  0.6 5.1 %collective-permute-start.2 = (bf16[64,1536]{1,0:T(8,128)(2,1)}, bf16[64,1536]{1,0:T(8,128)(2,1)S(1)}, u32[]{:S(2)}, u32[]{:S(2)}) collective-permute-start(bf16[64,1536]{1,0:T(8,128)(2,1)} %refs_13_.1), channel_id=1, source_target_pairs={{0,3},{1,0},{2,1},{3,2},{4,7},{5,4},{6,5},{7,6},{8,11},{9,8},{10,9... | collective-permute-start | bytes 589832 | tf_op jit(solution)/shard_map/ppermute | solution.py:548
  9.1 7.0 %shard_map.93 = (bf16[8,256,768]{2,1,0:T(8,128)(2,1)S(1)}, bf16[8,256,768]{2,1,0:T(8,128)(2,1)S(1)}, bf16[8,256,768]{2,1,0:T(8,128)(2,1)S(1)}, bf16[8,256,768]{2...) custom-call(bf16[1536,6144]{1,0:T(8,128)(2,1)} %weight_ref.2, ...), custom_call_target="tpu_custom_call" | custom-call | flops 9437 | bytes 37748 | tf_op jit(solution)/shard_map/pallas_call | solution.py:261
  16.1 7.3 %shard_map.94 = (bf16[8,768,256]{2,1,0:T(8,128)(2,1)S(1)}, bf16[8,768,256]{2,1,0:T(8,128)(2,1)S(1)}, bf16[8,768,256]{2,1,0:T(8,128)(2,1)S(1)}, bf16[8,768,256]{2...) custom-call(bf16[6144,1536]{1,0:T(8,128)(2,1)} %weight_ref.3, ...), custom_call_target="tpu_custom_call" | custom-call | flops 9437 | bytes 37748 | tf_op jit(solution)/shard_map/pallas_call | solution.py:261
  23.4 2.9 %collective-permute-start.4 = (bf16[64,1536]{1,0:T(8,128)(2,1)S(1)}, bf16[64,1536]{1,0:T(8,128)(2,1)S(1)}, u32[]{:S(2)}, u32[]{:S(2)}) collective-permute-start(bf16[64,1536]{1,0:T(8,128)(2,1)S(1)} %copy-done), channel_id=1, source_target_pairs={{0,3},{1,0},{2,1},{3,2},{4,7},{5,4},{6,5},{7,6},{8,11},{9,8},{10,9... | collective-permute-start | bytes 589832 | tf_op jit(solution)/shard_map/ppermute | solution.py:548
  26.3 7.2 %shard_map.95 = (bf16[4,256,768]{2,1,0:T(8,128)(2,1)S(1)}, bf16[4,256,768]{2,1,0:T(8,128)(2,1)S(1)}) custom-call(s32[16]{0:T(128)S(1)} %stack.46.table_ref, bf16[64,1536]{1,0:T(8,128)(2,1)S(1)} %copy-done.1, bf16[64,1536]{1,0:T(8,128)(2,1)S(1)} %collective-permute-done.refs_1_.refs_14_, bf16[64,1536]{1,0:T(8,128)(2,1)S(1)} %collective-permute-done.1.refs_2_.refs_15_, ...), custom_call_target="tpu_custom_call" | custom-call | flops 4831838 | bytes 22806 | tf_op jit(solution)/shard_map/pallas_call | solution.py:320
  33.6 1.7 %collective-permute-done.3.refs_1_.refs_2_.refs_3_ = bf16[64,1536]{1,0:T(8,128)(2,1)S(1)} collective-permute-done((bf16[64,1536]{1,0:T(8,128)(2,1)S(1)}, bf16[64,1536]{1,0:T(8,128)(2,1)S(1)}, u32[]{:S(2)}, u32[]{:S(2)}) %collective-permute-start.3) | collective-permute-done | bytes 196640 | tf_op jit(solution)/shard_map/ppermute | solution.py:548
  35.3 3.4 %collective-permute-done.5.got_ref = bf16[4,256,768]{2,1,0:T(8,128)(2,1)S(1)} collective-permute-done((bf16[4,256,768]{2,1,0:T(8,128)(2,1)S(1)}, bf16[4,256,768]{2,1,0:T(8,128)(2,1)S(1)}, u32[]{:S(2)}, u32[]{:S(2)}) %collective-permute-start.5) | collective-permute-done | bytes 1572896 | tf_op jit(solution)/shard_map/ppermute | solution.py:538
  42.6 6.6 %collective-permute-done.7.refs_2_.refs_3_.refs_4_ = bf16[64,1536]{1,0:T(8,128)(2,1)S(1)} collective-permute-done((bf16[64,1536]{1,0:T(8,128)(2,1)S(1)}, bf16[64,1536]{1,0:T(8,128)(2,1)S(1)}, u32[]{:S(2)}, u32[]{:S(2)}) %collective-permute-start.7) | collective-permute-done | bytes 196640 | tf_op jit(solution)/shard_map/ppermute | solution.py:551
  49.2 1.9 %collective-permute-done.6.near_ref = bf16[2,256,768]{2,1,0:T(8,128)(2,1)S(1)} collective-permute-done((bf16[2,256,768]{2,1,0:T(8,128)(2,1)S(1)}, bf16[2,256,768]{2,1,0:T(8,128)(2,1)S(1)}, u32[]{:S(2)}, u32[]{:S(2)}) %collective-permute-start.6) | collective-permute-done | bytes 786464 | tf_op jit(solution)/shard_map/ppermute | solution.py:541
  52.8 7.5 %shard_map.98 = (bf16[4,256,768]{2,1,0:T(8,128)(2,1)S(1)}, bf16[4,256,768]{2,1,0:T(8,128)(2,1)S(1)}) custom-call(s32[16]{0:T(128)S(1)} %stack.46.table_ref, bf16[64,1536]{1,0:T(8,128)(2,1)S(1)} %copy-done, bf16[64,1536]{1,0:T(8,128)(2,1)S(1)} %collective-permute-done.3.refs_1_.refs_2_.refs_3_, ...), custom_call_target="tpu_custom_call" | custom-call | flops 4831838 | bytes 22806 | tf_op jit(solution)/shard_map/pallas_call | solution.py:320
  65.7 2.9 %collective-permute-done.12.right_ref = bf16[256,768]{1,0:T(8,128)(2,1)S(1)} collective-permute-done((bf16[256,768]{1,0:T(8,128)(2,1)S(1)}, bf16[256,768]{1,0:T(8,128)(2,1)S(1)}, u32[]{:S(2)}, u32[]{:S(2)}) %collective-permute-start.12) | collective-permute-done | bytes 393248 | tf_op jit(solution)/shard_map/ppermute | solution.py:541
  69.3 3.8 %shard_map.102.refs_7_ = bf16[6144,1536]{1,0:T(8,128)(2,1)} custom-call(s32[16]{0:T(128)S(1)} %stack.46.table_ref, bf16[2,256,768]{2,1,0:T(8,128)(2,1)S(1)} %shard_map.101.refs_0_, bf16[64,1536]{1,0:T(8,128)(2,1)S(1)} %copy-done, bf16[64,1536]{1,0:T(8,128)(2,1)S(1)} %collective-permute-done.3.refs_1_.refs_2_.refs_3_, ...), custom_call_target="tpu_custom_call" | custom-call | flops 1207959 | bytes 5505 | tf_op jit(solution)/shard_map/pallas_call | solution.py:526
  73.0 9.1 %collective-permute-done.11.near_ref = bf16[2,256,768]{2,1,0:T(8,128)(2,1)S(1)} collective-permute-done((bf16[2,256,768]{2,1,0:T(8,128)(2,1)S(1)}, bf16[2,256,768]{2,1,0:T(8,128)(2,1)S(1)}, u32[]{:S(2)}, u32[]{:S(2)}) %collective-permute-start.11) | collective-permute-done | bytes 786464 | tf_op jit(solution)/shard_map/ppermute | solution.py:541
  82.9 4.0 %shard_map.104.refs_8_ = f32[256,1536]{1,0:T(8,128)S(1)} custom-call(s32[16]{0:T(128)S(1)} %stack.46.table_ref, bf16[2,256,768]{2,1,0:T(8,128)(2,1)S(1)} %shard_map.101.refs_0_, bf16[2,256,768]{2,1,0:T(8,128)(2,1)S(1)} %collective-permute-done.14.refs_1_.refs_0_, bf16[8,768,256]{2,1,0:T(8,128)(2,1)S(1)} %get-tuple-element.123.refs_5_.refs_2_, ...), custom_call_target="tpu_custom_call" | custom-call | flops 2415919 | bytes 12582 | tf_op jit(solution)/shard_map/pallas_call | solution.py:403
  86.8 3.8 %shard_map.105.refs_8_ = bf16[6144,1536]{1,0:T(8,128)(2,1)} custom-call(s32[16]{0:T(128)S(1)} %stack.46.table_ref, bf16[2,256,768]{2,1,0:T(8,128)(2,1)S(1)} %collective-permute-done.14.refs_1_.refs_0_, bf16[64,1536]{1,0:T(8,128)(2,1)S(1)} %copy-done, ...), custom_call_target="tpu_custom_call", output_to_operand_aliasing={{}: (8, {})} | custom-call | flops 1207959 | bytes 5505 | tf_op jit(solution)/shard_map/pallas_call | solution.py:526
  93.0 4.1 %shard_map.107 = (bf16[64,1536]{1,0:T(8,128)(2,1)S(1)}, bf16[64,1536]{1,0:T(8,128)(2,1)S(1)}, bf16[64,1536]{1,0:T(8,128)(2,1)S(1)}, bf16[64,1536]{1,0:T(8,128)(2,1)S(1)}) custom-call(s32[16]{0:T(128)S(1)} %stack.46.table_ref, bf16[2,256,768]{2,1,0:T(8,128)(2,1)S(1)} %collective-permute-done.16.refs_0_, ...), custom_call_target="tpu_custom_call" | custom-call | flops 2415919 | bytes 12582 | tf_op jit(solution)/shard_map/pallas_call | solution.py:403
  97.0 2.1 %collective-permute-done.15.right_ref = bf16[256,768]{1,0:T(8,128)(2,1)S(1)} collective-permute-done((bf16[256,768]{1,0:T(8,128)(2,1)S(1)}, bf16[256,768]{1,0:T(8,128)(2,1)S(1)}, u32[]{:S(2)}, u32[]{:S(2)}) %collective-permute-start.15) | collective-permute-done | bytes 393248 | tf_op jit(solution)/shard_map/ppermute | solution.py:541
  101.5 3.9 %collective-permute-start.19 = (bf16[64,1536]{1,0:T(8,128)(2,1)S(1)}, bf16[64,1536]{1,0:T(8,128)(2,1)S(1)}, u32[]{:S(2)}, u32[]{:S(2)}) collective-permute-start(bf16[64,1536]{1,0:T(8,128)(2,1)S(1)} %get-tuple-element.178), channel_id=1, source_target_pairs={{0,1},{1,2},{4,5},{5,6},{8,9},{9,10},{12,13},{13,14},{16,17},{17,1... | collective-permute-start | bytes 589832 | tf_op jit(solution)/shard_map/ppermute | solution.py:551
  105.5 4.2 %shard_map.109.refs_8_ = f32[256,1536]{1,0:T(8,128)S(1)} custom-call(s32[16]{0:T(128)S(1)} %stack.46.table_ref, bf16[2,256,768]{2,1,0:T(8,128)(2,1)S(1)} %shard_map.108.refs_0_.refs_9_, bf16[2,256,768]{2,1,0:T(8,128)(2,1)S(1)} %collective-permute-done.21.refs_1_.refs_10_, bf16[8,256,768]{2,1,0:T(8,128)(2,1)S(1)} %get-tuple-element.125.refs_4_.refs_2_, ...), custom_call_target="tpu_custom_call" | custom-call | flops 2415919 | bytes 12582 | tf_op jit(solution)/shard_map/pallas_call | solution.py:403
  112.7 2.4 %collective-permute-start.23 = (bf16[64,1536]{1,0:T(8,128)(2,1)S(1)}, bf16[64,1536]{1,0:T(8,128)(2,1)S(1)}, u32[]{:S(2)}, u32[]{:S(2)}) collective-permute-start(bf16[64,1536]{1,0:T(8,128)(2,1)S(1)} %get-tuple-element.187), channel_id=1, source_target_pairs={{0,3},{1,0},{2,1},{3,2},{4,7},{5,4},{6,5},{7,6},{8,11},{9,8},{10,9... | collective-permute-start | bytes 589832 | tf_op jit(solution)/shard_map/ppermute | solution.py:548
  115.2 4.2 %shard_map.111 = (bf16[64,1536]{1,0:T(8,128)(2,1)S(1)}, bf16[64,1536]{1,0:T(8,128)(2,1)S(1)}, bf16[64,1536]{1,0:T(8,128)(2,1)S(1)}, bf16[64,1536]{1,0:T(8,128)(2,1)S(1)}) custom-call(s32[16]{0:T(128)S(1)} %stack.46.table_ref, bf16[2,256,768]{2,1,0:T(8,128)(2,1)S(1)} %collective-permute-done.18.refs_0_.refs_11_, ...), custom_call_target="tpu_custom_call" | custom-call | flops 2415919 | bytes 12582 | tf_op jit(solution)/shard_map/pallas_call | solution.py:403
  121.0 1.9 %collective-permute-start.27 = (bf16[64,1536]{1,0:T(8,128)(2,1)S(1)}, bf16[64,1536]{1,0:T(8,128)(2,1)S(1)}, u32[]{:S(2)}, u32[]{:S(2)}) collective-permute-start(bf16[64,1536]{1,0:T(8,128)(2,1)S(1)} %get-tuple-element.198), channel_id=1, source_target_pairs={{0,1},{1,2},{2,3},{3,0},{4,5},{5,6},{6,7},{7,4},{8,9},{9,10},{10,1... | collective-permute-start | bytes 589832 | tf_op jit(solution)/shard_map/ppermute | solution.py:548
  123.0 14.9 %shard_map.112 = (bf16[6144,1536]{1,0:T(8,128)(2,1)}, bf16[1536,6144]{1,0:T(8,128)(2,1)}) custom-call(s32[16]{0:T(128)S(1)} %stack.46.table_ref, bf16[2,256,768]{2,1,0:T(8,128)(2,1)S(1)} %collective-permute-done.16.refs_0_, bf16[2,256,768]{2,1,0:T(8,128)(2,1)S(1)} %collective-permute-done.17.refs_1_, ...), custom_call_target="tpu_custom_call", output_to_operand_aliasing={{0}: (9, {})} | custom-call | flops 7247757 | bytes 33030 | tf_op jit(solution)/shard_map/pallas_call | solution.py:526
  137.8 3.7 %collective-permute-done.26.refs_5_ = bf16[64,1536]{1,0:T(8,128)(2,1)S(1)} collective-permute-done((bf16[64,1536]{1,0:T(8,128)(2,1)S(1)}, bf16[64,1536]{1,0:T(8,128)(2,1)S(1)}, u32[]{:S(2)}, u32[]{:S(2)}) %collective-permute-start.26) | collective-permute-done | bytes 196640 | tf_op jit(solution)/shard_map/ppermute | solution.py:548
  (66 shorter events, 25.9 us)
Async XLA Ops:
  0.6 22.8 %collective-permute-start.2 = (bf16[64,1536]{1,0:T(8,128)(2,1)}, bf16[64,1536]{1,0:T(8,128)(2,1)S(1)}, u32[]{:S(2)}, u32[]{:S(2)}) collective-permute-start(bf16[64,1536]{1,0:T(8,128)(2,1)} %refs_13_.1), channel_id=1, source_target_pairs={{0,3},{1,0},{2,1},{3,2},{4,7},{5,4},{6,5},{7,6},{8,11},{9,8},{10,9... | collective-permute-start | bytes 589832 | tf_op jit(solution)/shard_map/ppermute | solution.py:548
  5.7 17.7 %collective-permute-start.1 = (bf16[64,1536]{1,0:T(8,128)(2,1)}, bf16[64,1536]{1,0:T(8,128)(2,1)S(1)}, u32[]{:S(2)}, u32[]{:S(2)}) collective-permute-start(bf16[64,1536]{1,0:T(8,128)(2,1)} %refs_13_.1), channel_id=1, source_target_pairs={{0,2},{1,3},{2,0},{3,1},{4,6},{5,7},{6,4},{7,5},{8,10},{9,11},{10,... | collective-permute-start | bytes 589832 | tf_op jit(solution)/shard_map/ppermute | solution.py:548
  5.7 17.7 %collective-permute-start = (bf16[64,1536]{1,0:T(8,128)(2,1)}, bf16[64,1536]{1,0:T(8,128)(2,1)S(1)}, u32[]{:S(2)}, u32[]{:S(2)}) collective-permute-start(bf16[64,1536]{1,0:T(8,128)(2,1)} %refs_13_.1), channel_id=1, source_target_pairs={{0,1},{1,2},{2,3},{3,0},{4,5},{5,6},{6,7},{7,4},{8,9},{9,10},{10,1... | collective-permute-start | bytes 589832 | tf_op jit(solution)/shard_map/ppermute | solution.py:548
  23.4 10.1 %collective-permute-start.4 = (bf16[64,1536]{1,0:T(8,128)(2,1)S(1)}, bf16[64,1536]{1,0:T(8,128)(2,1)S(1)}, u32[]{:S(2)}, u32[]{:S(2)}) collective-permute-start(bf16[64,1536]{1,0:T(8,128)(2,1)S(1)} %copy-done), channel_id=1, source_target_pairs={{0,3},{1,0},{2,1},{3,2},{4,7},{5,4},{6,5},{7,6},{8,11},{9,8},{10,9... | collective-permute-start | bytes 589832 | tf_op jit(solution)/shard_map/ppermute | solution.py:548
  26.3 8.9 %collective-permute-start.3 = (bf16[64,1536]{1,0:T(8,128)(2,1)S(1)}, bf16[64,1536]{1,0:T(8,128)(2,1)S(1)}, u32[]{:S(2)}, u32[]{:S(2)}) collective-permute-start(bf16[64,1536]{1,0:T(8,128)(2,1)S(1)} %copy-done), channel_id=1, source_target_pairs={{0,1},{1,2},{2,3},{3,0},{4,5},{5,6},{6,7},{7,4},{8,9},{9,10},{10,1... | collective-permute-start | bytes 589832 | tf_op jit(solution)/shard_map/ppermute | solution.py:548
  39.1 12.1 %collective-permute-start.6 = (bf16[2,256,768]{2,1,0:T(8,128)(2,1)S(1)}, bf16[2,256,768]{2,1,0:T(8,128)(2,1)S(1)}, u32[]{:S(2)}, u32[]{:S(2)}) collective-permute-start(bf16[2,256,768]{2,1,0:T(8,128)(2,1)S(1)} %get-tuple-element.136), channel_id=1, source_target_pairs={{0,8},{4,20},{8,0},{12,28},{16,24},{20,4},{24,16},{28,12},{1,9},{5... | collective-permute-start | bytes 2359304 | tf_op jit(solution)/shard_map/ppermute | solution.py:541
  40.6 8.6 %collective-permute-start.7 = (bf16[64,1536]{1,0:T(8,128)(2,1)S(1)}, bf16[64,1536]{1,0:T(8,128)(2,1)S(1)}, u32[]{:S(2)}, u32[]{:S(2)}) collective-permute-start(bf16[64,1536]{1,0:T(8,128)(2,1)S(1)} %collective-permute-done.4.refs_4_.refs_5_.refs_6_), channel_id=1, source_target_pairs={{1,0},{2,1},{5,4},{6,5},{9,8},{10,9},{13,12},{14,13},{17,16},{18,1... | collective-permute-start | bytes 589832 | tf_op jit(solution)/shard_map/ppermute | solution.py:551
  41.9 7.3 %collective-permute-start.8 = (bf16[64,1536]{1,0:T(8,128)(2,1)S(1)}, bf16[64,1536]{1,0:T(8,128)(2,1)S(1)}, u32[]{:S(2)}, u32[]{:S(2)}) collective-permute-start(bf16[64,1536]{1,0:T(8,128)(2,1)S(1)} %collective-permute-done.3.refs_1_.refs_2_.refs_3_), channel_id=1, source_target_pairs={{1,2},{2,3},{5,6},{6,7},{9,10},{10,11},{13,14},{14,15},{17,18},{18... | collective-permute-start | bytes 589832 | tf_op jit(solution)/shard_map/ppermute | solution.py:551
  51.3 9.1 %collective-permute-start.9 = (bf16[256,768]{1,0:T(8,128)(2,1)S(1)}, bf16[256,768]{1,0:T(8,128)(2,1)S(1)}, u32[]{:S(2)}, u32[]{:S(2)}) collective-permute-start(bf16[256,768]{1,0:T(8,128)(2,1)S(1)} %get-tuple-element.141), channel_id=1, source_target_pairs={{0,16},{4,12},{8,24},{12,4},{16,0},{20,28},{24,8},{28,20},{1,17},{... | collective-permute-start | bytes 1179656 | tf_op jit(solution)/shard_map/ppermute | solution.py:545
  60.7 7.8 %collective-permute-start.12 = (bf16[256,768]{1,0:T(8,128)(2,1)S(1)}, bf16[256,768]{1,0:T(8,128)(2,1)S(1)}, u32[]{:S(2)}, u32[]{:S(2)}) collective-permute-start(bf16[256,768]{1,0:T(8,128)(2,1)S(1)} %get-tuple-element.155.left_ref), channel_id=1, source_target_pairs={{0,8},{4,20},{8,0},{12,28},{16,24},{20,4},{24,16},{28,12},{1,9},{5... | collective-permute-start | bytes 1179656 | tf_op jit(solution)/shard_map/ppermute | solution.py:541
  64.2 18.0 %collective-permute-start.11 = (bf16[2,256,768]{2,1,0:T(8,128)(2,1)S(1)}, bf16[2,256,768]{2,1,0:T(8,128)(2,1)S(1)}, u32[]{:S(2)}, u32[]{:S(2)}) collective-permute-start(bf16[2,256,768]{2,1,0:T(8,128)(2,1)S(1)} %get-tuple-element.159), channel_id=1, source_target_pairs={{0,8},{4,20},{8,0},{12,28},{16,24},{20,4},{24,16},{28,12},{1,9},{5... | collective-permute-start | bytes 2359304 | tf_op jit(solution)/shard_map/ppermute | solution.py:541
  68.6 14.2 %collective-permute-start.14 = (bf16[2,256,768]{2,1,0:T(8,128)(2,1)S(1)}, bf16[2,256,768]{2,1,0:T(8,128)(2,1)S(1)}, u32[]{:S(2)}, u32[]{:S(2)}) collective-permute-start(bf16[2,256,768]{2,1,0:T(8,128)(2,1)S(1)} %shard_map.101.refs_0_), channel_id=1, source_target_pairs={{0,4},{4,0},{8,12},{12,8},{16,20},{20,16},{24,28},{28,24},{1,5},{5... | collective-permute-start | bytes 2359304 | tf_op jit(solution)/shard_map/ppermute | solution.py:538
  68.7 21.9 %collective-permute-start.16 = (bf16[2,256,768]{2,1,0:T(8,128)(2,1)S(1)}, bf16[2,256,768]{2,1,0:T(8,128)(2,1)S(1)}, u32[]{:S(2)}, u32[]{:S(2)}) collective-permute-start(bf16[2,256,768]{2,1,0:T(8,128)(2,1)S(1)} %shard_map.101.refs_0_), channel_id=1, source_target_pairs={{0,16},{4,12},{8,24},{12,4},{16,0},{20,28},{24,8},{28,20},{1,17},{... | collective-permute-start | bytes 2359304 | tf_op jit(solution)/shard_map/ppermute | solution.py:545
  82.3 8.3 %collective-permute-start.13 = (bf16[256,768]{1,0:T(8,128)(2,1)S(1)}, bf16[256,768]{1,0:T(8,128)(2,1)S(1)}, u32[]{:S(2)}, u32[]{:S(2)}) collective-permute-start(bf16[256,768]{1,0:T(8,128)(2,1)S(1)} %get-tuple-element.164), channel_id=1, source_target_pairs={{0,16},{4,12},{8,24},{12,4},{16,0},{20,28},{24,8},{28,20},{1,17},{... | collective-permute-start | bytes 1179656 | tf_op jit(solution)/shard_map/ppermute | solution.py:545
  91.3 7.8 %collective-permute-start.15 = (bf16[256,768]{1,0:T(8,128)(2,1)S(1)}, bf16[256,768]{1,0:T(8,128)(2,1)S(1)}, u32[]{:S(2)}, u32[]{:S(2)}) collective-permute-start(bf16[256,768]{1,0:T(8,128)(2,1)S(1)} %shard_map.106.left_ref), channel_id=1, source_target_pairs={{0,8},{4,20},{8,0},{12,28},{16,24},{20,4},{24,16},{28,12},{1,9},{5... | collective-permute-start | bytes 1179656 | tf_op jit(solution)/shard_map/ppermute | solution.py:541
  99.2 6.3 %collective-permute-start.21 = (bf16[2,256,768]{2,1,0:T(8,128)(2,1)S(1)}, bf16[2,256,768]{2,1,0:T(8,128)(2,1)S(1)}, u32[]{:S(2)}, u32[]{:S(2)}) collective-permute-start(bf16[2,256,768]{2,1,0:T(8,128)(2,1)S(1)} %shard_map.108.refs_0_.refs_9_), channel_id=1, source_target_pairs={{0,4},{4,0},{8,12},{12,8},{16,20},{20,16},{24,28},{28,24},{1,5},{5... | collective-permute-start | bytes 2359304 | tf_op jit(solution)/shard_map/ppermute | solution.py:538
  99.3 12.1 %collective-permute-start.18 = (bf16[2,256,768]{2,1,0:T(8,128)(2,1)S(1)}, bf16[2,256,768]{2,1,0:T(8,128)(2,1)S(1)}, u32[]{:S(2)}, u32[]{:S(2)}) collective-permute-start(bf16[2,256,768]{2,1,0:T(8,128)(2,1)S(1)} %shard_map.108.refs_0_.refs_9_), channel_id=1, source_target_pairs={{0,16},{4,12},{8,24},{12,4},{16,0},{20,28},{24,8},{28,20},{1,17},{... | collective-permute-start | bytes 2359304 | tf_op jit(solution)/shard_map/ppermute | solution.py:545
  100.9 8.8 %collective-permute-start.20 = (bf16[64,1536]{1,0:T(8,128)(2,1)S(1)}, bf16[64,1536]{1,0:T(8,128)(2,1)S(1)}, u32[]{:S(2)}, u32[]{:S(2)}) collective-permute-start(bf16[64,1536]{1,0:T(8,128)(2,1)S(1)} %get-tuple-element.178), channel_id=1, source_target_pairs={{2,1},{3,2},{6,5},{7,6},{10,9},{11,10},{14,13},{15,14},{18,17},{19... | collective-permute-start | bytes 589832 | tf_op jit(solution)/shard_map/ppermute | solution.py:551
  101.5 8.4 %collective-permute-start.19 = (bf16[64,1536]{1,0:T(8,128)(2,1)S(1)}, bf16[64,1536]{1,0:T(8,128)(2,1)S(1)}, u32[]{:S(2)}, u32[]{:S(2)}) collective-permute-start(bf16[64,1536]{1,0:T(8,128)(2,1)S(1)} %get-tuple-element.178), channel_id=1, source_target_pairs={{0,1},{1,2},{4,5},{5,6},{8,9},{9,10},{12,13},{13,14},{16,17},{17,1... | collective-permute-start | bytes 589832 | tf_op jit(solution)/shard_map/ppermute | solution.py:551
  111.3 26.5 %collective-permute-start.22 = (bf16[64,1536]{1,0:T(8,128)(2,1)S(1)}, bf16[64,1536]{1,0:T(8,128)(2,1)S(1)}, u32[]{:S(2)}, u32[]{:S(2)}) collective-permute-start(bf16[64,1536]{1,0:T(8,128)(2,1)S(1)} %get-tuple-element.186), channel_id=1, source_target_pairs={{0,1},{1,2},{2,3},{3,0},{4,5},{5,6},{6,7},{7,4},{8,9},{9,10},{10,1... | collective-permute-start | bytes 589832 | tf_op jit(solution)/shard_map/ppermute | solution.py:548
  112.7 25.1 %collective-permute-start.23 = (bf16[64,1536]{1,0:T(8,128)(2,1)S(1)}, bf16[64,1536]{1,0:T(8,128)(2,1)S(1)}, u32[]{:S(2)}, u32[]{:S(2)}) collective-permute-start(bf16[64,1536]{1,0:T(8,128)(2,1)S(1)} %get-tuple-element.187), channel_id=1, source_target_pairs={{0,3},{1,0},{2,1},{3,2},{4,7},{5,4},{6,5},{7,6},{8,11},{9,8},{10,9... | collective-permute-start | bytes 589832 | tf_op jit(solution)/shard_map/ppermute | solution.py:548
  119.4 18.5 %collective-permute-start.25 = (bf16[64,1536]{1,0:T(8,128)(2,1)S(1)}, bf16[64,1536]{1,0:T(8,128)(2,1)S(1)}, u32[]{:S(2)}, u32[]{:S(2)}) collective-permute-start(bf16[64,1536]{1,0:T(8,128)(2,1)S(1)} %get-tuple-element.196), channel_id=1, source_target_pairs={{0,3},{1,0},{2,1},{3,2},{4,7},{5,4},{6,5},{7,6},{8,11},{9,8},{10,9... | collective-permute-start | bytes 589832 | tf_op jit(solution)/shard_map/ppermute | solution.py:548
  120.3 21.3 %collective-permute-start.26 = (bf16[64,1536]{1,0:T(8,128)(2,1)S(1)}, bf16[64,1536]{1,0:T(8,128)(2,1)S(1)}, u32[]{:S(2)}, u32[]{:S(2)}) collective-permute-start(bf16[64,1536]{1,0:T(8,128)(2,1)S(1)} %get-tuple-element.197), channel_id=1, source_target_pairs={{0,2},{1,3},{2,0},{3,1},{4,6},{5,7},{6,4},{7,5},{8,10},{9,11},{10,... | collective-permute-start | bytes 589832 | tf_op jit(solution)/shard_map/ppermute | solution.py:548
  121.0 20.5 %collective-permute-start.27 = (bf16[64,1536]{1,0:T(8,128)(2,1)S(1)}, bf16[64,1536]{1,0:T(8,128)(2,1)S(1)}, u32[]{:S(2)}, u32[]{:S(2)}) collective-permute-start(bf16[64,1536]{1,0:T(8,128)(2,1)S(1)} %get-tuple-element.198), channel_id=1, source_target_pairs={{0,1},{1,2},{2,3},{3,0},{4,5},{5,6},{6,7},{7,4},{8,9},{9,10},{10,1... | collective-permute-start | bytes 589832 | tf_op jit(solution)/shard_map/ppermute | solution.py:548
  (6 other events, 30.6 us)

commit v3 on v2

--- a/solution.py
+++ b/solution.py
@@ -82,6 +82,7 @@
 
 AT_SENT, AT_HELD, AT_NEAR, AT_FAR = 0, 4, 8, 12
 AT_NEAR_CORE = 10
+AT_ODD = 16
 
 
 def spans(length):
@@ -89,7 +90,7 @@
     return [slice(lo, lo + span) for lo in range(0, length, span)]
 
 
-def share_table(row):
+def share_table(row, col):
     first = jnp.where(row % 2 == 0, X, Y)
     second = (X | Y) - first
     other = row ^ CORE
@@ -97,7 +98,7 @@
     held = [row ^ first ^ second, row ^ first, row ^ second, row]
     near = [row, row ^ first, other, other ^ second]
     far = [row ^ second, row ^ second ^ first, other ^ first, other ^ first ^ second]
-    return jnp.stack(sent + held + near + far)
+    return jnp.stack(sent + held + near + far + [col % 2])
 
 
 def cost(flops, moved):
@@ -199,14 +200,45 @@
     return small(body, [((2,) + left.shape, BF16)], left, right)[0]
 
 
-def added_pairs(*pairs):
-    def body(*refs):
-        given, outs = refs[: 2 * len(pairs)], refs[2 * len(pairs) :]
-        for n, out in enumerate(outs):
-            left, right = given[2 * n : 2 * n + 2]
-            out[...] = (left[...].astype(F32) + right[...].astype(F32)).astype(BF16)
-
-    return small(body, [(left.shape, BF16) for left, _ in pairs], *flat(pairs))
+def by_place(body, table, outs, *given):
+    return pl.pallas_call(
+        body,
+        out_shape=tuple(pltpu.VMEM(shape, BF16) for shape in outs),
+        in_specs=[pl.BlockSpec(memory_space=pltpu.SMEM)] + [resident()] * len(given),
+        out_specs=tuple(resident() for _ in outs),
+        compiler_params=pltpu.CompilerParams(vmem_limit_bytes=VMEM_LIMIT),
+    )(table, *[in_vmem(array) for array in given])
+
+
+def chosen(table, odd, even):
+    def body(table_ref, odd_ref, even_ref, out):
+        @pl.when(table_ref[AT_ODD] == 1)
+        def _():
+            out[...] = odd_ref[...]
+
+        @pl.when(table_ref[AT_ODD] == 0)
+        def _():
+            out[...] = even_ref[...]
+
+    return by_place(body, table, [odd.shape], odd, even)[0]
+
+
+def joined(table, upper, lower, hop):
+    def body(table_ref, upper_ref, lower_ref, hop_ref, to_upper, to_lower):
+        def join(out, ref):
+            out[...] = (ref[...].astype(F32) + hop_ref[...].astype(F32)).astype(BF16)
+
+        @pl.when(table_ref[AT_ODD] == 1)
+        def _():
+            join(to_upper, upper_ref)
+            to_lower[...] = lower_ref[...]
+
+        @pl.when(table_ref[AT_ODD] == 0)
+        def _():
+            join(to_lower, lower_ref)
+            to_upper[...] = upper_ref[...]
+
+    return by_place(body, table, [upper.shape] * 2, upper, lower, hop)
 
 
 def added(*sums):
@@ -528,7 +560,7 @@
 
 def per_device_tuned(n_row, n_col, inputs, w_up, w_down, mask_up, mask_down, cotangent):
     share = w_up.shape[1] // n_row
-    table = share_table(lax.axis_index("row"))
+    table = share_table(lax.axis_index("row"), lax.axis_index("col"))
     keep_up = jnp.repeat(mask_up.astype(BF16), TILE, axis=1)
     keep_up = keep_up.reshape(-1, n_row, share).transpose(1, 0, 2)
     keep_down = jnp.repeat(mask_down.astype(BF16), TILE, axis=1)
@@ -547,11 +579,11 @@
     def along_col(value, shift):
         return lax.ppermute(value, "col", [(i, (i + shift) % n_col) for i in range(n_col)])
 
-    def toward(value, step, froms):
-        return lax.ppermute(value, "col", [(i, i + step) for i in froms])
+    def between_places(value):
+        return lax.ppermute(value, "col", [(i, i ^ 1) for i in range(n_col)])
 
     def relayed(lower, upper):
-        return toward(upper, -1, (1, 2)), toward(lower, 1, (1, 2))
+        return between_places(chosen(table, upper, lower))
 
     def after(value, *done):
         return lax.optimization_barrier((value, *done))[0]
@@ -581,8 +613,8 @@
     pair, rest = add_cores(up_held, up_got)
 
     near = along_first(pair)
-    near, far_lower, far_upper = together(near, *far)
-    cot_all = [(cotangent,), (lower,), (far_lower, far_upper), (upper,)]
+    near, far = together(near, far)
+    cot_all = [(cotangent,), (lower,), (far,), (upper,)]
     passed, own = add_first(rest, near)
     last = along_second(passed)
     back_sent, back_held = project(
@@ -621,13 +653,13 @@
         after(table, grad), AT_FAR, [act_far, act_far_core], down, True, out_total, n_col
     )
     grad_first, *out_blocks = together(grad_first, *out_blocks)
-    hops = toward(out_blocks[2], 1, (0, 1)), toward(out_blocks[2], -1, (2, 3))
+    hop = between_places(out_blocks[2])
     grad_near = paired(grad, grad_first)
     grad_far = along_second(grad_near)
     grad_core = between_cores(grad_near)
     in_total = gathered(table, AT_NEAR, [grad_near, grad_core], up, False)
-    *hops, in_total = together(*hops, in_total)
-    to_upper, to_lower = added_pairs((out_blocks[3], hops[0]), (out_blocks[1], hops[1]))
+    hop, in_total = together(hop, in_total)
+    to_upper, to_lower = joined(table, out_blocks[3], out_blocks[1], hop)
     grad_far, in_total, to_upper, to_lower = together(
         grad_far, in_total, to_upper, to_lower
     )

time: 143 us -> 143 us (level)
  starting transfers between devices: 33.7 us -> 28.9 us
  waiting for transfers between devices: 34.6 us -> 38.2 us
    ppermute x4 -> x2, starting transfers between devices: 6.55 us -> 2.87 us  [between_places(): return lax.ppermute(value, 'col', [(i, i ^ 1) for i in range(n_col)])]
    ppermute x4, waiting for transfers between devices: 1.35 us -> 2.94 us  [along_second(): lax.ppermute(value, 'row', [(i, i ^ second[i]) for i in range(n_row)])]
    ppermute x4 -> x2, waiting for transfers between devices: 6.84 us -> 6.65 us  [between_places(): return lax.ppermute(value, 'col', [(i, i ^ 1) for i in range(n_col)])]
  transfers between devices with their start and end apart: 28 -> 26, of which waited for: 12 -> 12; matrix products, arithmetic and copies ran while one was open for 2% -> 2% of each run, Pallas kernels for 49% -> 49%
where the time goes in v3:
time: 143 us; the launch traced here: 142 us
  Pallas kernels  71.9 us (50%)
  waiting for transfers between devices  38.2 us (27%)
  starting transfers between devices  28.9 us (20%)
    pallas_call x3, Pallas kernels, weight_gradients(): return outs(table, *flat([job.arrays for job in jobs]))  22.3 us
    ppermute x4, waiting for transfers between devices, along_first(): lax.ppermute(value, 'row', [(i, i ^ first_of(i)) for i in range(n_row)])  17.2 us
    pallas_call x4, Pallas kernels, gathered(): return call(table, *pairs, *map(in_vmem, kept), *given)  16.4 us
    ppermute x10, starting transfers between devices, along_col(): lax.ppermute(value, 'col', [(i, (i + shift) % n_col) for i in range(n_col)])  15.3 us
    pallas_call x2, Pallas kernels, project(): return call(table, *flat(parts), *map(in_vmem, kept))  14.7 us
    pallas_call x2, Pallas kernels, kept_pieces(): pl.pallas_call(body, out_shape=(pltpu.VMEM((shares,) + block, BF16),) * l...  14.3 us
    ppermute x2, waiting for transfers between devices, between_places(): return lax.ppermute(value, 'col', [(i, i ^ 1) for i in range(n_col)])  6.65 us
    ppermute x10, waiting for transfers between devices, along_col(): lax.ppermute(value, 'col', [(i, (i + shift) % n_col) for i in range(n_col)])  6.33 us
  transfers between devices with their start and end apart: 26, of which 12 were waited for; matrix products, arithmetic and copies ran while one was open for 2% of the time, Pallas kernels for 49%

profile of v3, /device:TPU:0, one launch (start us, length us, event | category | flops | bytes accessed | tf_op | source)
XLA Modules:
  0.0 142.3 jit_solution(16167776257998280799)
XLA Ops:
  0.6 5.1 %collective-permute-start.2 = (bf16[64,1536]{1,0:T(8,128)(2,1)}, bf16[64,1536]{1,0:T(8,128)(2,1)S(1)}, u32[]{:S(2)}, u32[]{:S(2)}) collective-permute-start(bf16[64,1536]{1,0:T(8,128)(2,1)} %refs_12_.1), channel_id=1, source_target_pairs={{0,3},{1,0},{2,1},{3,2},{4,7},{5,4},{6,5},{7,6},{8,11},{9,8},{10,9... | collective-permute-start | bytes 589832 | tf_op jit(solution)/shard_map/ppermute | solution.py:580
  9.1 7.0 %shard_map.93 = (bf16[8,256,768]{2,1,0:T(8,128)(2,1)S(1)}, bf16[8,256,768]{2,1,0:T(8,128)(2,1)S(1)}, bf16[8,256,768]{2,1,0:T(8,128)(2,1)S(1)}, bf16[8,256,768]{2...) custom-call(bf16[1536,6144]{1,0:T(8,128)(2,1)} %weight_ref.2, ...), custom_call_target="tpu_custom_call" | custom-call | flops 9437 | bytes 37748 | tf_op jit(solution)/shard_map/pallas_call | solution.py:293
  16.1 7.3 %shard_map.94 = (bf16[8,768,256]{2,1,0:T(8,128)(2,1)S(1)}, bf16[8,768,256]{2,1,0:T(8,128)(2,1)S(1)}, bf16[8,768,256]{2,1,0:T(8,128)(2,1)S(1)}, bf16[8,768,256]{2...) custom-call(bf16[6144,1536]{1,0:T(8,128)(2,1)} %weight_ref.3, ...), custom_call_target="tpu_custom_call" | custom-call | flops 9437 | bytes 37748 | tf_op jit(solution)/shard_map/pallas_call | solution.py:293
  23.5 2.9 %collective-permute-start.4 = (bf16[64,1536]{1,0:T(8,128)(2,1)S(1)}, bf16[64,1536]{1,0:T(8,128)(2,1)S(1)}, u32[]{:S(2)}, u32[]{:S(2)}) collective-permute-start(bf16[64,1536]{1,0:T(8,128)(2,1)S(1)} %copy-done), channel_id=1, source_target_pairs={{0,3},{1,0},{2,1},{3,2},{4,7},{5,4},{6,5},{7,6},{8,11},{9,8},{10,9... | collective-permute-start | bytes 589832 | tf_op jit(solution)/shard_map/ppermute | solution.py:580
  26.3 7.2 %shard_map.95 = (bf16[4,256,768]{2,1,0:T(8,128)(2,1)S(1)}, bf16[4,256,768]{2,1,0:T(8,128)(2,1)S(1)}) custom-call(s32[17]{0:T(128)S(1)} %stack.50.table_ref, bf16[64,1536]{1,0:T(8,128)(2,1)S(1)} %copy-done.1, bf16[64,1536]{1,0:T(8,128)(2,1)S(1)} %collective-permute-done.refs_1_.refs_13_, bf16[64,1536]{1,0:T(8,128)(2,1)S(1)} %collective-permute-done.1.refs_2_.refs_14_, ...), custom_call_target="tpu_custom_call" | custom-call | flops 4831838 | bytes 22806 | tf_op jit(solution)/shard_map/pallas_call | solution.py:352
  33.6 1.7 %collective-permute-done.3.even_ref.refs_1_.refs_2_.refs_3_ = bf16[64,1536]{1,0:T(8,128)(2,1)S(1)} collective-permute-done((bf16[64,1536]{1,0:T(8,128)(2,1)S(1)}, bf16[64,1536]{1,0:T(8,128)(2,1)S(1)}, u32[]{:S(2)}, u32[]{:S(2)}) %collective-permute-start.3) | collective-permute-done | bytes 196640 | tf_op jit(solution)/shard_map/ppermute | solution.py:580
  35.3 3.4 %collective-permute-done.5.got_ref = bf16[4,256,768]{2,1,0:T(8,128)(2,1)S(1)} collective-permute-done((bf16[4,256,768]{2,1,0:T(8,128)(2,1)S(1)}, bf16[4,256,768]{2,1,0:T(8,128)(2,1)S(1)}, u32[]{:S(2)}, u32[]{:S(2)}) %collective-permute-start.5) | collective-permute-done | bytes 1572896 | tf_op jit(solution)/shard_map/ppermute | solution.py:570
  42.7 5.3 %collective-permute-done.7.refs_2_.refs_3_.refs_4_ = bf16[64,1536]{1,0:T(8,128)(2,1)S(1)} collective-permute-done((bf16[64,1536]{1,0:T(8,128)(2,1)S(1)}, bf16[64,1536]{1,0:T(8,128)(2,1)S(1)}, u32[]{:S(2)}, u32[]{:S(2)}) %collective-permute-start.7) | collective-permute-done | bytes 196640 | tf_op jit(solution)/shard_map/ppermute | solution.py:583
  48.0 3.2 %collective-permute-done.6.near_ref = bf16[2,256,768]{2,1,0:T(8,128)(2,1)S(1)} collective-permute-done((bf16[2,256,768]{2,1,0:T(8,128)(2,1)S(1)}, bf16[2,256,768]{2,1,0:T(8,128)(2,1)S(1)}, u32[]{:S(2)}, u32[]{:S(2)}) %collective-permute-start.6) | collective-permute-done | bytes 786464 | tf_op jit(solution)/shard_map/ppermute | solution.py:573
  51.3 1.6 %collective-permute-start.8 = (bf16[256,768]{1,0:T(8,128)(2,1)S(1)}, bf16[256,768]{1,0:T(8,128)(2,1)S(1)}, u32[]{:S(2)}, u32[]{:S(2)}) collective-permute-start(bf16[256,768]{1,0:T(8,128)(2,1)S(1)} %get-tuple-element.139), channel_id=1, source_target_pairs={{0,16},{4,12},{8,24},{12,4},{16,0},{20,28},{24,8},{28,20},{1,17},{... | collective-permute-start | bytes 1179656 | tf_op jit(solution)/shard_map/ppermute | solution.py:577
  52.9 7.5 %shard_map.99 = (bf16[4,256,768]{2,1,0:T(8,128)(2,1)S(1)}, bf16[4,256,768]{2,1,0:T(8,128)(2,1)S(1)}) custom-call(s32[17]{0:T(128)S(1)} %stack.50.table_ref, bf16[64,1536]{1,0:T(8,128)(2,1)S(1)} %copy-done, bf16[64,1536]{1,0:T(8,128)(2,1)S(1)} %collective-permute-done.3.even_ref.refs_1_.refs_2_.refs_3_, ...), custom_call_target="tpu_custom_call" | custom-call | flops 4831838 | bytes 22806 | tf_op jit(solution)/shard_map/pallas_call | solution.py:352
  65.8 2.9 %collective-permute-done.11.right_ref = bf16[256,768]{1,0:T(8,128)(2,1)S(1)} collective-permute-done((bf16[256,768]{1,0:T(8,128)(2,1)S(1)}, bf16[256,768]{1,0:T(8,128)(2,1)S(1)}, u32[]{:S(2)}, u32[]{:S(2)}) %collective-permute-start.11) | collective-permute-done | bytes 393248 | tf_op jit(solution)/shard_map/ppermute | solution.py:573
  69.4 3.7 %shard_map.103.refs_6_ = bf16[6144,1536]{1,0:T(8,128)(2,1)} custom-call(s32[17]{0:T(128)S(1)} %stack.50.table_ref, bf16[2,256,768]{2,1,0:T(8,128)(2,1)S(1)} %shard_map.102.refs_0_, bf16[64,1536]{1,0:T(8,128)(2,1)S(1)} %copy-done, bf16[64,1536]{1,0:T(8,128)(2,1)S(1)} %collective-permute-done.3.even_ref.refs_1_.refs_2_.refs_3_, ...), custom_call_target="tpu_custom_call" | custom-call | flops 1207959 | bytes 5505 | tf_op jit(solution)/shard_map/pallas_call | solution.py:558
  73.1 9.1 %collective-permute-done.10.near_ref = bf16[2,256,768]{2,1,0:T(8,128)(2,1)S(1)} collective-permute-done((bf16[2,256,768]{2,1,0:T(8,128)(2,1)S(1)}, bf16[2,256,768]{2,1,0:T(8,128)(2,1)S(1)}, u32[]{:S(2)}, u32[]{:S(2)}) %collective-permute-start.10) | collective-permute-done | bytes 786464 | tf_op jit(solution)/shard_map/ppermute | solution.py:573
  82.9 4.0 %shard_map.105.refs_8_ = f32[256,1536]{1,0:T(8,128)S(1)} custom-call(s32[17]{0:T(128)S(1)} %stack.50.table_ref, bf16[2,256,768]{2,1,0:T(8,128)(2,1)S(1)} %shard_map.102.refs_0_, bf16[2,256,768]{2,1,0:T(8,128)(2,1)S(1)} %collective-permute-done.13.refs_1_.refs_0_, bf16[8,768,256]{2,1,0:T(8,128)(2,1)S(1)} %get-tuple-element.121.refs_4_.refs_2_, ...), custom_call_target="tpu_custom_call" | custom-call | flops 2415919 | bytes 12582 | tf_op jit(solution)/shard_map/pallas_call | solution.py:435
  86.9 3.8 %shard_map.106.refs_7_ = bf16[6144,1536]{1,0:T(8,128)(2,1)} custom-call(s32[17]{0:T(128)S(1)} %stack.50.table_ref, bf16[2,256,768]{2,1,0:T(8,128)(2,1)S(1)} %collective-permute-done.13.refs_1_.refs_0_, bf16[64,1536]{1,0:T(8,128)(2,1)S(1)} %copy-done, ...), custom_call_target="tpu_custom_call", output_to_operand_aliasing={{}: (7, {})} | custom-call | flops 1207959 | bytes 5505 | tf_op jit(solution)/shard_map/pallas_call | solution.py:558
  93.0 4.1 %shard_map.108 = (bf16[64,1536]{1,0:T(8,128)(2,1)S(1)}, bf16[64,1536]{1,0:T(8,128)(2,1)S(1)}, bf16[64,1536]{1,0:T(8,128)(2,1)S(1)}, bf16[64,1536]{1,0:T(8,128)(2,1)S(1)}) custom-call(s32[17]{0:T(128)S(1)} %stack.50.table_ref, bf16[2,256,768]{2,1,0:T(8,128)(2,1)S(1)} %collective-permute-done.15.refs_0_, ...), custom_call_target="tpu_custom_call" | custom-call | flops 2415919 | bytes 12582 | tf_op jit(solution)/shard_map/pallas_call | solution.py:435
  97.1 2.1 %collective-permute-done.14.right_ref = bf16[256,768]{1,0:T(8,128)(2,1)S(1)} collective-permute-done((bf16[256,768]{1,0:T(8,128)(2,1)S(1)}, bf16[256,768]{1,0:T(8,128)(2,1)S(1)}, u32[]{:S(2)}, u32[]{:S(2)}) %collective-permute-start.14) | collective-permute-done | bytes 393248 | tf_op jit(solution)/shard_map/ppermute | solution.py:573
  102.3 4.2 %shard_map.110.refs_8_ = f32[256,1536]{1,0:T(8,128)S(1)} custom-call(s32[17]{0:T(128)S(1)} %stack.50.table_ref, bf16[2,256,768]{2,1,0:T(8,128)(2,1)S(1)} %shard_map.109.refs_0_.refs_8_, bf16[2,256,768]{2,1,0:T(8,128)(2,1)S(1)} %collective-permute-done.19.refs_1_.refs_9_, bf16[8,256,768]{2,1,0:T(8,128)(2,1)S(1)} %get-tuple-element.123.refs_4_.refs_2_, ...), custom_call_target="tpu_custom_call" | custom-call | flops 2415919 | bytes 12582 | tf_op jit(solution)/shard_map/pallas_call | solution.py:435
  108.5 2.9 %collective-permute-done.17.refs_0_.refs_10_ = bf16[2,256,768]{2,1,0:T(8,128)(2,1)S(1)} collective-permute-done((bf16[2,256,768]{2,1,0:T(8,128)(2,1)S(1)}, bf16[2,256,768]{2,1,0:T(8,128)(2,1)S(1)}, u32[]{:S(2)}, u32[]{:S(2)}) %collective-permute-start.17) | collective-permute-done | bytes 786464 | tf_op jit(solution)/shard_map/ppermute | solution.py:577
  112.8 2.4 %collective-permute-start.21 = (bf16[64,1536]{1,0:T(8,128)(2,1)S(1)}, bf16[64,1536]{1,0:T(8,128)(2,1)S(1)}, u32[]{:S(2)}, u32[]{:S(2)}) collective-permute-start(bf16[64,1536]{1,0:T(8,128)(2,1)S(1)} %get-tuple-element.183), channel_id=1, source_target_pairs={{0,3},{1,0},{2,1},{3,2},{4,7},{5,4},{6,5},{7,6},{8,11},{9,8},{10,9... | collective-permute-start | bytes 589832 | tf_op jit(solution)/shard_map/ppermute | solution.py:580
  115.2 4.2 %shard_map.112 = (bf16[64,1536]{1,0:T(8,128)(2,1)S(1)}, bf16[64,1536]{1,0:T(8,128)(2,1)S(1)}, bf16[64,1536]{1,0:T(8,128)(2,1)S(1)}, bf16[64,1536]{1,0:T(8,128)(2,1)S(1)}) custom-call(s32[17]{0:T(128)S(1)} %stack.50.table_ref, bf16[2,256,768]{2,1,0:T(8,128)(2,1)S(1)} %collective-permute-done.17.refs_0_.refs_10_, ...), custom_call_target="tpu_custom_call" | custom-call | flops 2415919 | bytes 12582 | tf_op jit(solution)/shard_map/pallas_call | solution.py:435
  121.9 14.8 %shard_map.113 = (bf16[6144,1536]{1,0:T(8,128)(2,1)}, bf16[1536,6144]{1,0:T(8,128)(2,1)}) custom-call(s32[17]{0:T(128)S(1)} %stack.50.table_ref, bf16[2,256,768]{2,1,0:T(8,128)(2,1)S(1)} %collective-permute-done.15.refs_0_, bf16[2,256,768]{2,1,0:T(8,128)(2,1)S(1)} %collective-permute-done.16.refs_1_, ...), custom_call_target="tpu_custom_call", output_to_operand_aliasing={{0}: (8, {})} | custom-call | flops 7247757 | bytes 33030 | tf_op jit(solution)/shard_map/pallas_call | solution.py:558
  136.8 4.6 %collective-permute-done.24.refs_5_ = bf16[64,1536]{1,0:T(8,128)(2,1)S(1)} collective-permute-done((bf16[64,1536]{1,0:T(8,128)(2,1)S(1)}, bf16[64,1536]{1,0:T(8,128)(2,1)S(1)}, u32[]{:S(2)}, u32[]{:S(2)}) %collective-permute-start.24) | collective-permute-done | bytes 196640 | tf_op jit(solution)/shard_map/ppermute | solution.py:580
  (63 shorter events, 26.4 us)
Async XLA Ops:
  0.6 22.8 %collective-permute-start.2 = (bf16[64,1536]{1,0:T(8,128)(2,1)}, bf16[64,1536]{1,0:T(8,128)(2,1)S(1)}, u32[]{:S(2)}, u32[]{:S(2)}) collective-permute-start(bf16[64,1536]{1,0:T(8,128)(2,1)} %refs_12_.1), channel_id=1, source_target_pairs={{0,3},{1,0},{2,1},{3,2},{4,7},{5,4},{6,5},{7,6},{8,11},{9,8},{10,9... | collective-permute-start | bytes 589832 | tf_op jit(solution)/shard_map/ppermute | solution.py:580
  5.7 17.7 %collective-permute-start.1 = (bf16[64,1536]{1,0:T(8,128)(2,1)}, bf16[64,1536]{1,0:T(8,128)(2,1)S(1)}, u32[]{:S(2)}, u32[]{:S(2)}) collective-permute-start(bf16[64,1536]{1,0:T(8,128)(2,1)} %refs_12_.1), channel_id=1, source_target_pairs={{0,2},{1,3},{2,0},{3,1},{4,6},{5,7},{6,4},{7,5},{8,10},{9,11},{10,... | collective-permute-start | bytes 589832 | tf_op jit(solution)/shard_map/ppermute | solution.py:580
  5.7 17.7 %collective-permute-start = (bf16[64,1536]{1,0:T(8,128)(2,1)}, bf16[64,1536]{1,0:T(8,128)(2,1)S(1)}, u32[]{:S(2)}, u32[]{:S(2)}) collective-permute-start(bf16[64,1536]{1,0:T(8,128)(2,1)} %refs_12_.1), channel_id=1, source_target_pairs={{0,1},{1,2},{2,3},{3,0},{4,5},{5,6},{6,7},{7,4},{8,9},{9,10},{10,1... | collective-permute-start | bytes 589832 | tf_op jit(solution)/shard_map/ppermute | solution.py:580
  23.5 10.1 %collective-permute-start.4 = (bf16[64,1536]{1,0:T(8,128)(2,1)S(1)}, bf16[64,1536]{1,0:T(8,128)(2,1)S(1)}, u32[]{:S(2)}, u32[]{:S(2)}) collective-permute-start(bf16[64,1536]{1,0:T(8,128)(2,1)S(1)} %copy-done), channel_id=1, source_target_pairs={{0,3},{1,0},{2,1},{3,2},{4,7},{5,4},{6,5},{7,6},{8,11},{9,8},{10,9... | collective-permute-start | bytes 589832 | tf_op jit(solution)/shard_map/ppermute | solution.py:580
  26.3 8.9 %collective-permute-start.3 = (bf16[64,1536]{1,0:T(8,128)(2,1)S(1)}, bf16[64,1536]{1,0:T(8,128)(2,1)S(1)}, u32[]{:S(2)}, u32[]{:S(2)}) collective-permute-start(bf16[64,1536]{1,0:T(8,128)(2,1)S(1)} %copy-done), channel_id=1, source_target_pairs={{0,1},{1,2},{2,3},{3,0},{4,5},{5,6},{6,7},{7,4},{8,9},{9,10},{10,1... | collective-permute-start | bytes 589832 | tf_op jit(solution)/shard_map/ppermute | solution.py:580
  35.3 3.4 %collective-permute-start.5 = (bf16[4,256,768]{2,1,0:T(8,128)(2,1)S(1)}, bf16[4,256,768]{2,1,0:T(8,128)(2,1)S(1)}, u32[]{:S(2)}, u32[]{:S(2)}) collective-permute-start(bf16[4,256,768]{2,1,0:T(8,128)(2,1)S(1)} %get-tuple-element.132), channel_id=1, source_target_pairs={{0,4},{4,0},{8,12},{12,8},{16,20},{20,16},{24,28},{28,24},{1,5},{5... | collective-permute-start | bytes 4718600 | tf_op jit(solution)/shard_map/ppermute | solution.py:570
  39.1 12.1 %collective-permute-start.6 = (bf16[2,256,768]{2,1,0:T(8,128)(2,1)S(1)}, bf16[2,256,768]{2,1,0:T(8,128)(2,1)S(1)}, u32[]{:S(2)}, u32[]{:S(2)}) collective-permute-start(bf16[2,256,768]{2,1,0:T(8,128)(2,1)S(1)} %get-tuple-element.134), channel_id=1, source_target_pairs={{0,8},{4,20},{8,0},{12,28},{16,24},{20,4},{24,16},{28,12},{1,9},{5... | collective-permute-start | bytes 2359304 | tf_op jit(solution)/shard_map/ppermute | solution.py:573
  41.2 6.8 %collective-permute-start.7 = (bf16[64,1536]{1,0:T(8,128)(2,1)S(1)}, bf16[64,1536]{1,0:T(8,128)(2,1)S(1)}, u32[]{:S(2)}, u32[]{:S(2)}) collective-permute-start(bf16[64,1536]{1,0:T(8,128)(2,1)S(1)} %shard_map.97), channel_id=1, source_target_pairs={{0,1},{1,0},{2,3},{3,2},{4,5},{5,4},{6,7},{7,6},{8,9},{9,8},{10,11... | collective-permute-start | bytes 589832 | tf_op jit(solution)/shard_map/ppermute | solution.py:583
  51.3 9.1 %collective-permute-start.8 = (bf16[256,768]{1,0:T(8,128)(2,1)S(1)}, bf16[256,768]{1,0:T(8,128)(2,1)S(1)}, u32[]{:S(2)}, u32[]{:S(2)}) collective-permute-start(bf16[256,768]{1,0:T(8,128)(2,1)S(1)} %get-tuple-element.139), channel_id=1, source_target_pairs={{0,16},{4,12},{8,24},{12,4},{16,0},{20,28},{24,8},{28,20},{1,17},{... | collective-permute-start | bytes 1179656 | tf_op jit(solution)/shard_map/ppermute | solution.py:577
  60.4 3.5 %collective-permute-start.9 = (bf16[4,256,768]{2,1,0:T(8,128)(2,1)S(1)}, bf16[4,256,768]{2,1,0:T(8,128)(2,1)S(1)}, u32[]{:S(2)}, u32[]{:S(2)}) collective-permute-start(bf16[4,256,768]{2,1,0:T(8,128)(2,1)S(1)} %get-tuple-element.154), channel_id=1, source_target_pairs={{0,4},{4,0},{8,12},{12,8},{16,20},{20,16},{24,28},{28,24},{1,5},{5... | collective-permute-start | bytes 4718600 | tf_op jit(solution)/shard_map/ppermute | solution.py:570
  60.8 7.8 %collective-permute-start.11 = (bf16[256,768]{1,0:T(8,128)(2,1)S(1)}, bf16[256,768]{1,0:T(8,128)(2,1)S(1)}, u32[]{:S(2)}, u32[]{:S(2)}) collective-permute-start(bf16[256,768]{1,0:T(8,128)(2,1)S(1)} %get-tuple-element.152.left_ref), channel_id=1, source_target_pairs={{0,8},{4,20},{8,0},{12,28},{16,24},{20,4},{24,16},{28,12},{1,9},{5... | collective-permute-start | bytes 1179656 | tf_op jit(solution)/shard_map/ppermute | solution.py:573
  64.2 18.0 %collective-permute-start.10 = (bf16[2,256,768]{2,1,0:T(8,128)(2,1)S(1)}, bf16[2,256,768]{2,1,0:T(8,128)(2,1)S(1)}, u32[]{:S(2)}, u32[]{:S(2)}) collective-permute-start(bf16[2,256,768]{2,1,0:T(8,128)(2,1)S(1)} %get-tuple-element.156), channel_id=1, source_target_pairs={{0,8},{4,20},{8,0},{12,28},{16,24},{20,4},{24,16},{28,12},{1,9},{5... | collective-permute-start | bytes 2359304 | tf_op jit(solution)/shard_map/ppermute | solution.py:573
  68.7 14.2 %collective-permute-start.13 = (bf16[2,256,768]{2,1,0:T(8,128)(2,1)S(1)}, bf16[2,256,768]{2,1,0:T(8,128)(2,1)S(1)}, u32[]{:S(2)}, u32[]{:S(2)}) collective-permute-start(bf16[2,256,768]{2,1,0:T(8,128)(2,1)S(1)} %shard_map.102.refs_0_), channel_id=1, source_target_pairs={{0,4},{4,0},{8,12},{12,8},{16,20},{20,16},{24,28},{28,24},{1,5},{5... | collective-permute-start | bytes 2359304 | tf_op jit(solution)/shard_map/ppermute | solution.py:570
  68.8 21.9 %collective-permute-start.15 = (bf16[2,256,768]{2,1,0:T(8,128)(2,1)S(1)}, bf16[2,256,768]{2,1,0:T(8,128)(2,1)S(1)}, u32[]{:S(2)}, u32[]{:S(2)}) collective-permute-start(bf16[2,256,768]{2,1,0:T(8,128)(2,1)S(1)} %shard_map.102.refs_0_), channel_id=1, source_target_pairs={{0,16},{4,12},{8,24},{12,4},{16,0},{20,28},{24,8},{28,20},{1,17},{... | collective-permute-start | bytes 2359304 | tf_op jit(solution)/shard_map/ppermute | solution.py:577
  82.3 8.3 %collective-permute-start.12 = (bf16[256,768]{1,0:T(8,128)(2,1)S(1)}, bf16[256,768]{1,0:T(8,128)(2,1)S(1)}, u32[]{:S(2)}, u32[]{:S(2)}) collective-permute-start(bf16[256,768]{1,0:T(8,128)(2,1)S(1)} %get-tuple-element.161), channel_id=1, source_target_pairs={{0,16},{4,12},{8,24},{12,4},{16,0},{20,28},{24,8},{28,20},{1,17},{... | collective-permute-start | bytes 1179656 | tf_op jit(solution)/shard_map/ppermute | solution.py:577
  91.4 7.8 %collective-permute-start.14 = (bf16[256,768]{1,0:T(8,128)(2,1)S(1)}, bf16[256,768]{1,0:T(8,128)(2,1)S(1)}, u32[]{:S(2)}, u32[]{:S(2)}) collective-permute-start(bf16[256,768]{1,0:T(8,128)(2,1)S(1)} %shard_map.107.left_ref), channel_id=1, source_target_pairs={{0,8},{4,20},{8,0},{12,28},{16,24},{20,4},{24,16},{28,12},{1,9},{5... | collective-permute-start | bytes 1179656 | tf_op jit(solution)/shard_map/ppermute | solution.py:573
  99.3 12.1 %collective-permute-start.17 = (bf16[2,256,768]{2,1,0:T(8,128)(2,1)S(1)}, bf16[2,256,768]{2,1,0:T(8,128)(2,1)S(1)}, u32[]{:S(2)}, u32[]{:S(2)}) collective-permute-start(bf16[2,256,768]{2,1,0:T(8,128)(2,1)S(1)} %shard_map.109.refs_0_.refs_8_), channel_id=1, source_target_pairs={{0,16},{4,12},{8,24},{12,4},{16,0},{20,28},{24,8},{28,20},{1,17},{... | collective-permute-start | bytes 2359304 | tf_op jit(solution)/shard_map/ppermute | solution.py:577
  100.9 6.9 %collective-permute-start.18 = (bf16[64,1536]{1,0:T(8,128)(2,1)S(1)}, bf16[64,1536]{1,0:T(8,128)(2,1)S(1)}, u32[]{:S(2)}, u32[]{:S(2)}) collective-permute-start(bf16[64,1536]{1,0:T(8,128)(2,1)S(1)} %get-tuple-element.175), channel_id=1, source_target_pairs={{0,1},{1,0},{2,3},{3,2},{4,5},{5,4},{6,7},{7,6},{8,9},{9,8},{10,11... | collective-permute-start | bytes 589832 | tf_op jit(solution)/shard_map/ppermute | solution.py:583
  111.4 3.8 %collective-permute-start.22 = (bf16[2,256,768]{2,1,0:T(8,128)(2,1)S(1)}, bf16[2,256,768]{2,1,0:T(8,128)(2,1)S(1)}, u32[]{:S(2)}, u32[]{:S(2)}) collective-permute-start(bf16[2,256,768]{2,1,0:T(8,128)(2,1)S(1)} %collective-permute-done.17.refs_0_.refs_10_), channel_id=1, source_target_pairs={{0,4},{4,0},{8,12},{12,8},{16,20},{20,16},{24,28},{28,24},{1,5},{5... | collective-permute-start | bytes 2359304 | tf_op jit(solution)/shard_map/ppermute | solution.py:570
  111.4 25.4 %collective-permute-start.20 = (bf16[64,1536]{1,0:T(8,128)(2,1)S(1)}, bf16[64,1536]{1,0:T(8,128)(2,1)S(1)}, u32[]{:S(2)}, u32[]{:S(2)}) collective-permute-start(bf16[64,1536]{1,0:T(8,128)(2,1)S(1)} %get-tuple-element.182), channel_id=1, source_target_pairs={{0,1},{1,2},{2,3},{3,0},{4,5},{5,6},{6,7},{7,4},{8,9},{9,10},{10,1... | collective-permute-start | bytes 589832 | tf_op jit(solution)/shard_map/ppermute | solution.py:580
  112.8 24.0 %collective-permute-start.21 = (bf16[64,1536]{1,0:T(8,128)(2,1)S(1)}, bf16[64,1536]{1,0:T(8,128)(2,1)S(1)}, u32[]{:S(2)}, u32[]{:S(2)}) collective-permute-start(bf16[64,1536]{1,0:T(8,128)(2,1)S(1)} %get-tuple-element.183), channel_id=1, source_target_pairs={{0,3},{1,0},{2,1},{3,2},{4,7},{5,4},{6,5},{7,6},{8,11},{9,8},{10,9... | collective-permute-start | bytes 589832 | tf_op jit(solution)/shard_map/ppermute | solution.py:580
  119.5 17.3 %collective-permute-start.23 = (bf16[64,1536]{1,0:T(8,128)(2,1)S(1)}, bf16[64,1536]{1,0:T(8,128)(2,1)S(1)}, u32[]{:S(2)}, u32[]{:S(2)}) collective-permute-start(bf16[64,1536]{1,0:T(8,128)(2,1)S(1)} %get-tuple-element.192), channel_id=1, source_target_pairs={{0,3},{1,0},{2,1},{3,2},{4,7},{5,4},{6,5},{7,6},{8,11},{9,8},{10,9... | collective-permute-start | bytes 589832 | tf_op jit(solution)/shard_map/ppermute | solution.py:580
  120.2 21.2 %collective-permute-start.24 = (bf16[64,1536]{1,0:T(8,128)(2,1)S(1)}, bf16[64,1536]{1,0:T(8,128)(2,1)S(1)}, u32[]{:S(2)}, u32[]{:S(2)}) collective-permute-start(bf16[64,1536]{1,0:T(8,128)(2,1)S(1)} %get-tuple-element.193), channel_id=1, source_target_pairs={{0,2},{1,3},{2,0},{3,1},{4,6},{5,7},{6,4},{7,5},{8,10},{9,11},{10,... | collective-permute-start | bytes 589832 | tf_op jit(solution)/shard_map/ppermute | solution.py:580
  120.8 20.6 %collective-permute-start.25 = (bf16[64,1536]{1,0:T(8,128)(2,1)S(1)}, bf16[64,1536]{1,0:T(8,128)(2,1)S(1)}, u32[]{:S(2)}, u32[]{:S(2)}) collective-permute-start(bf16[64,1536]{1,0:T(8,128)(2,1)S(1)} %get-tuple-element.194), channel_id=1, source_target_pairs={{0,1},{1,2},{2,3},{3,0},{4,5},{5,6},{6,7},{7,4},{8,9},{9,10},{10,1... | collective-permute-start | bytes 589832 | tf_op jit(solution)/shard_map/ppermute | solution.py:580
  (4 other events, 23.0 us)
